TPU v7x, 512 devices: a whole 4x8x8 slice. The times are simulated.
512 devices in a mesh: cuts: 16 (over y, core), tile: 32 (over z, x).
Axes of the slice: x: 4, y: 8, z: 8, core: 2. Of those that a mesh axis runs over, the one named last changes fastest.
Arguments:
- obj_real: float32 [16, 4096, 256], P('cuts', 'tile'), may hold values from 0.9 to 1.1
- obj_imag: float32 [16, 4096, 256], P('cuts', 'tile'), may hold values from -0.4 to 0.4
- probe_real: float32 [128, 128], replicated, may hold values from -3.5 to 3.5
- probe_imag: float32 [128, 128], replicated, may hold values from -3.5 to 3.5
- prop_phase: float32 [128], replicated, may hold values from -3.140625 to 3.140625
- intensity: float32 [512, 128, 128], P('tile'), may hold values from 0 to 2
- offsets: int32 [512, 2], P('tile'), may hold values from 0 to 128, as said below
- counts: int32 [32], P('tile'), may hold values from 1 to 16, as said below
Outputs:
- object_grad: float32 [2, 16, 4096, 256], P(None, 'cuts', 'tile')
- probe_grad: float32 [2, 128, 128], P(None, 'cuts')
Inputs may be any that keep to these rules, and one draw needn't show every extreme that they name: `offsets`: column 0 lies in 0 to 127 and column 1 in 0 to 128; the upper ends are reached in every draw. `counts`: every tile has at least one live slot and some tile has all 16 slots live.
All inputs are finite; a program needn't handle non-finite values.
Results may differ from a plain program's by a relative error of at most 0.0003.
Values sent between devices are 32-bit elements; how exact they have to be, the bound alone decides.
No kernel may reach another device: no remote copies, remote signals or barrier semaphores. Data moves between devices by JAX's collectives and lax.ppermute only.
A program may use at most 64 MiB of HBM per device.

v0:
```python
import math

import jax
import jax.numpy as jnp
from jax import lax
from jax.sharding import PartitionSpec as P


def passed_along(block, axis, distance):
    devices = range(lax.axis_size(axis))
    route = [((i - distance) % len(devices), i) for i in devices]
    return lax.ppermute(block, axis, route)


def passed_along_2(value, axis, steps):
    count = lax.axis_size(axis)
    first, last = (max(0, -steps), min(count, count - steps))
    return lax.ppermute(value, axis, [(source, source + steps) for source in range(first, last)])


def mat_product(left_side, right_side):
    return jnp.dot(
        left_side, right_side, precision=lax.Precision.HIGHEST, preferred_element_type=jnp.float32
    )


def complex_product(left_side, right_side):
    return (
        mat_product(left_side[0], right_side[0]) - mat_product(left_side[1], right_side[1]),
        mat_product(left_side[0], right_side[1]) + mat_product(left_side[1], right_side[0]),
    )


def sandwich(before, current, after):
    return jnp.stack(complex_product(complex_product(before, (current[0], current[1])), after))


def pointwise(first_term, second_term):
    return jnp.stack(
        [
            first_term[0] * second_term[0] - first_term[1] * second_term[1],
            first_term[0] * second_term[1] + first_term[1] * second_term[0],
        ]
    )


def conj_pointwise(first_term, second_term):
    return jnp.stack(
        [
            first_term[0] * second_term[0] + first_term[1] * second_term[1],
            first_term[0] * second_term[1] - first_term[1] * second_term[0],
        ]
    )


def fourier_pair(patch_width):
    positions = jnp.arange(patch_width, dtype=jnp.int32)
    phase_table = (positions[:, None] * positions[None, :] % patch_width).astype(jnp.float32) * (
        2.0 * math.pi / patch_width
    )
    scale_factor = 1.0 / math.sqrt(patch_width)
    return (jnp.cos(phase_table) * scale_factor, -jnp.sin(phase_table) * scale_factor)


def build_operators(prop_phase, patch_width):
    fourier_real, fourier_imag = fourier_pair(patch_width)
    kernel_real = jnp.cos(prop_phase)[None, :]
    kernel_imag = jnp.sin(prop_phase)[None, :]
    left_side = (
        fourier_real * kernel_real + fourier_imag * kernel_imag,
        fourier_real * kernel_imag - fourier_imag * kernel_real,
    )
    spread_real, spread_imag = complex_product(left_side, (fourier_real, fourier_imag))
    return (
        (spread_real, spread_imag),
        (spread_real.T, spread_imag.T),
        (spread_real.T, -spread_imag.T),
        (spread_real, -spread_imag),
        (fourier_real, fourier_imag),
        (fourier_real, -fourier_imag),
    )


def take_patch(object_field, slice_index, row_start, col_start, patch_width):
    zero_index = jnp.zeros((), jnp.int32)
    starts = (zero_index, slice_index, row_start, col_start)
    return lax.dynamic_slice(object_field, starts, (2, 1, patch_width, patch_width))[:, 0]


def run_forward(object_field, start_wave, row_start, col_start, operators):
    patch_width = start_wave.shape[-1]

    def one_slice(current, slice_index):
        patch = take_patch(object_field, slice_index, row_start, col_start, patch_width)
        propagated = sandwich(operators[0], pointwise(current, patch), operators[1])
        return (propagated, current)

    return lax.scan(one_slice, start_wave, jnp.arange(object_field.shape[1], dtype=jnp.int32))


def run_backward(object_field, wave_stack, adjoint, row_start, col_start, operators):
    patch_width = adjoint.shape[-1]

    def one_slice(current, inputs):
        slice_index, stored_wave = inputs
        inner_grad = sandwich(operators[2], current, operators[3])
        patch = take_patch(object_field, slice_index, row_start, col_start, patch_width)
        return (conj_pointwise(patch, inner_grad), conj_pointwise(stored_wave, inner_grad))

    slice_ids = jnp.arange(object_field.shape[1], dtype=jnp.int32)
    return lax.scan(one_slice, adjoint, (slice_ids, wave_stack), reverse=True)


def exit_gradient(current, measured, operators):
    far_field = sandwich(operators[4], current, operators[4])
    excess = 2.0 * (far_field[0] * far_field[0] + far_field[1] * far_field[1] - measured)
    return sandwich(operators[5], far_field * excess[None], operators[5])


def add_patches(gradients, patch_grads, row_start, col_start):
    slice_count = patch_grads.shape[0]
    patch_width = patch_grads.shape[-1]
    zero_index = jnp.zeros((), jnp.int32)
    starts = (zero_index, zero_index, row_start, col_start)
    region = lax.dynamic_slice(gradients, starts, (2, slice_count, patch_width, patch_width))
    return lax.dynamic_update_slice(gradients, region + jnp.swapaxes(patch_grads, 0, 1), starts)


def per_device(obj_real, obj_imag, probe_real, probe_imag, prop_phase, intensity, offsets, counts):
    rows_own = obj_real.shape[1]
    patch_width = probe_real.shape[0]
    slot_total = intensity.shape[0]
    live_count = counts[0]
    operators = build_operators(prop_phase, patch_width)
    probe = jnp.stack([probe_real, probe_imag])
    zero_wave = jnp.zeros_like(probe)
    own_rows = jnp.stack([obj_real, obj_imag])
    below_rows = passed_along(own_rows, "tile", -1)
    object_field = jnp.concatenate([own_rows, below_rows], axis=2)
    section_count = lax.axis_size("cuts")
    section_index = lax.axis_index("cuts")
    slice_count = object_field.shape[1]
    zero_stack = jnp.zeros((slice_count, 2, patch_width, patch_width), jnp.float32)
    step_count = section_count + slot_total - 1

    def forward(step_index, loop_state):
        incoming, stored, exit_grads = loop_state
        slot_index = step_index - section_index
        in_range = (slot_index >= 0) & (slot_index < slot_total)
        slot_place = jnp.clip(slot_index, 0, slot_total - 1)
        row_start = offsets[slot_place, 0]
        col_start = offsets[slot_place, 1]
        start_wave = jnp.where(section_index == 0, probe, incoming)

        def finish(current):
            return exit_gradient(current, intensity[slot_place], operators)

        def skip_finish(current):
            return zero_wave

        def forward_active(current):
            outgoing, wave_stack = run_forward(
                object_field, current, row_start, col_start, operators
            )
            exit_term = lax.cond(section_index == section_count - 1, finish, skip_finish, outgoing)
            return (outgoing, wave_stack, exit_term)

        def forward_resting(current):
            return (zero_wave, zero_stack, zero_wave)

        outgoing, wave_stack, exit_term = lax.cond(
            in_range & (slot_index < live_count), forward_active, forward_resting, start_wave
        )
        stored = lax.dynamic_update_index_in_dim(
            stored, jnp.where(in_range, wave_stack, stored[slot_place]), slot_place, 0
        )
        exit_grads = lax.dynamic_update_index_in_dim(
            exit_grads, jnp.where(in_range, exit_term, exit_grads[slot_place]), slot_place, 0
        )
        return (passed_along_2(outgoing, "cuts", 1), stored, exit_grads)

    stored_init = jnp.zeros((slot_total, slice_count, 2, patch_width, patch_width), jnp.float32)
    exit_init = jnp.zeros((slot_total, 2, patch_width, patch_width), jnp.float32)
    forward_state = lax.fori_loop(0, step_count, forward, (zero_wave, stored_init, exit_init))
    stored = forward_state[1]
    exit_grads = forward_state[2]

    def backward(step_index, loop_state):
        incoming, gradients, probe_sum = loop_state
        slot_index = step_index - (section_count - 1 - section_index)
        in_range = (slot_index >= 0) & (slot_index < slot_total)
        slot_place = jnp.clip(slot_index, 0, slot_total - 1)
        row_start = offsets[slot_place, 0]
        col_start = offsets[slot_place, 1]
        start_wave = jnp.where(section_index == section_count - 1, exit_grads[slot_place], incoming)

        def backward_active(current):
            return run_backward(
                object_field, stored[slot_place], current, row_start, col_start, operators
            )

        def backward_resting(current):
            return (zero_wave, zero_stack)

        adjoint, patch_grads = lax.cond(
            in_range & (slot_index < live_count), backward_active, backward_resting, start_wave
        )
        gradients = add_patches(gradients, patch_grads, row_start, col_start)
        probe_sum = probe_sum + jnp.where(section_index == 0, adjoint, 0.0)
        return (passed_along_2(adjoint, "cuts", -1), gradients, probe_sum)

    backward_state = lax.fori_loop(
        0, step_count, backward, (zero_wave, jnp.zeros_like(object_field), zero_wave)
    )
    gradients = backward_state[1]
    probe_sum = backward_state[2]
    lower_band = passed_along(gradients[:, :, rows_own:], "tile", 1)
    object_grad = gradients[:, :, :rows_own] + lower_band
    tile_total = lax.psum(probe_sum, "tile")
    probe_grad = lax.psum_scatter(tile_total, "cuts", scatter_dimension=1, tiled=True)
    return (object_grad, probe_grad)


def solution(mesh):
    in_specs = (
        P("cuts", "tile", None),
        P("cuts", "tile", None),
        P(),
        P(),
        P(),
        P("tile", None, None),
        P("tile", None),
        P("tile"),
    )
    out_specs = (P(None, "cuts", "tile", None), P(None, "cuts", None))
    return jax.shard_map(
        per_device, mesh=mesh, in_specs=in_specs, out_specs=out_specs, check_vma=False
    )
```

profile of v0, /device:TPU:56, one launch (start us, length us, event | category | flops | bytes accessed | tf_op | source)
XLA Modules:
  0.0 1252.3 jit_solution(18108881514368085164)
XLA Ops:
  8.3 13.1 %collective-permute-start.2 = (f32[2,1,128,256]{3,2,1,0:T(8,128)S(1)}, f32[2,1,128,256]{3,2,1,0:T(8,128)S(1)}, u32[]{:S(2)}, u32[]{:S(2)}) collective-permute-start(f32[2,1,128,256]{3,2,1,0:T(8,128)S(1)} %pad_maximum_fusion.4), channel_id=1, source_target_pairs={{1,0},{2,1},{3,2},{4,3},{5,4},{6,5},{7,6},{8,7},{9,8},{10,9},{11,1... | collective-permute-start | bytes 786440 | tf_op jit(solution)/shard_map/ppermute | solution.py:12
  28.9 476.0 %while.50 = (s32[]{:T(128)}, f32[2,128,128]{2,1,0:T(8,128)S(1)}, f32[16,1,2,128,128]{4,3,2,1,0:T(8,128)}, f32[16,2,128,128]{3,2,1,0:T(8,128)S(1)}, s32[]{:T(128)...) while((s32[]{:T(128)}, f32[2,128,128]{2,1,0:T(8,128)S(1)}, ...), condition=%wide.region_5.6_spmd.clone.clone, body=%wide.region_0.5_spmd.clone.clone.sunk | while | flops 604880896 | bytes 9700654 | solution.py:184
  157.8 81.4 %collective-permute-done = f32[2,128,128]{2,1,0:T(8,128)S(1)} collective-permute-done((f32[2,128,128]{2,1,0:T(8,128)}, f32[2,128,128]{2,1,0:T(8,128)S(1)}, u32[]{:S(2)}, u32[]{:S(2)}) %collective-permute-start) | collective-permute-done | bytes 131104 | tf_op jit(solution)/shard_map/while/body/eval_jaxpr/ppermute | solution.py:18
  240.2 9.7 conditional.9
  258.6 9.7 conditional.9
  268.3 5.9 collective-permute-start
  278.7 9.7 conditional.9
  288.4 9.6 collective-permute-start
  302.4 9.7 conditional.9
  312.2 9.6 collective-permute-start
  326.2 9.7 conditional.9
  335.9 9.5 collective-permute-start
  349.9 9.7 conditional.9
  359.7 9.5 collective-permute-start
  373.6 9.7 conditional.9
  383.4 9.6 collective-permute-start
  399.4 17.3 %collective-permute-start = (f32[2,128,128]{2,1,0:T(8,128)}, f32[2,128,128]{2,1,0:T(8,128)S(1)}, u32[]{:S(2)}, u32[]{:S(2)}) collective-permute-start(f32[2,128,128]{2,1,0:T(8,128)} %get-tuple-element.1540), channel_id=1, source_target_pairs={{0,32},{32,64},{64,96},{96,128},{128,160},{160,192},{192,224},{224... | collective-permute-start | bytes 393224 | tf_op jit(solution)/shard_map/while/body/eval_jaxpr/ppermute | solution.py:18
  505.7 429.9 %while.51 = (s32[]{:T(128)}, f32[2,128,128]{2,1,0:T(8,128)S(1)}, f32[2,1,256,256]{3,2,0,1:T(8,128)}, f32[2,128,128]{2,1,0:T(8,128)S(1)}, s32[]{:T(128)}, /*index...) while((s32[]{:T(128)}, f32[2,128,128]{2,1,0:T(8,128)S(1)}, ...), condition=%wide.region_9.10_spmd.clone, body=%wide.region_6.9_spmd.clone.sunk | while | flops 201818128 | bytes 4850325 | solution.py:212
  513.9 3.4 dynamic_update_slice.44
  518.7 7.0 conditional.10
  532.5 3.4 dynamic_update_slice.44
  537.3 7.0 conditional.10
  551.1 3.6 dynamic_update_slice.44
  556.1 7.0 conditional.10
  569.9 3.6 dynamic_update_slice.44
  574.9 7.0 conditional.10
  588.7 3.6 dynamic_update_slice.44
  593.7 7.0 conditional.10
  607.5 3.6 dynamic_update_slice.44
  612.5 7.0 conditional.10
  626.3 3.6 dynamic_update_slice.44
  631.4 7.0 conditional.10
  645.2 3.6 dynamic_update_slice.44
  650.2 4.7 collective-permute-start.1
  659.8 3.5 dynamic_update_slice.44
  671.6 3.6 dynamic_update_slice.44
  683.4 3.6 dynamic_update_slice.44
  695.2 3.6 dynamic_update_slice.44
  700.2 4.5 collective-permute-start.1
  709.6 3.6 dynamic_update_slice.44
  721.4 3.4 dynamic_update_slice.44
  733.3 3.4 dynamic_update_slice.44
  744.9 3.6 dynamic_update_slice.44
  750.0 4.5 collective-permute-start.1
  759.3 3.4 dynamic_update_slice.44
  771.2 3.4 dynamic_update_slice.44
  782.7 3.4 dynamic_update_slice.44
  794.6 3.4 dynamic_update_slice.44
  799.4 5.7 collective-permute-start.1
  809.9 3.4 dynamic_update_slice.44
  821.8 3.4 dynamic_update_slice.44
  833.4 3.4 dynamic_update_slice.44
  845.2 3.4 dynamic_update_slice.44
  850.1 4.4 collective-permute-start.1
  859.3 3.4 dynamic_update_slice.44
  871.2 3.4 dynamic_update_slice.44
  894.7 3.4 dynamic_update_slice.44
  899.5 4.4 collective-permute-start.1
  908.8 3.4 dynamic_update_slice.44
  920.7 3.4 dynamic_update_slice.44
  932.2 3.4 dynamic_update_slice.44
  938.7 12.0 collective-permute-done.3
  952.3 215.6 %reduce-scatter.2.cloned.1.call-done = f32[2,8,128]{2,1,0:T(8,128)} async-done(((f32[2,128,128]{2,1,0:T(8,128)}), f32[2,8,128]{2,1,0:T(8,128)}) %reduce-scatter.2.cloned.1.call-update) | async-done | bytes 8208 | tf_op jit(solution)/shard_map/reduce_scatter | solution.py:220
  1168.0 77.4 %psum.8 = f32[2,8,128]{2,1,0:T(8,128)} all-reduce(f32[2,8,128]{2,1,0:T(8,128)} %reduce-scatter.2.cloned.1.call-done), channel_id=1, replica_groups=mesh['cuts'=16,'tile'=32] {'tile'}, use_global_device_ids=true, to_apply=%region_10.11 | all-reduce | flops 2048 | bytes 16384 | tf_op jit(solution)/shard_map/psum | solution.py:219
  (776 shorter events, 474.6 us)
Async XLA Ops:
  7.2 1160.8 %reduce-scatter.2.cloned.1.call-start = ((), (), s32[]{:S(2)}) async-start(), calls=%async_computation.1 | async-start | bytes 139264 | tf_op jit(solution)/shard_map/reduce_scatter | solution.py:220
  8.3 18.7 %collective-permute-start.2 = (f32[2,1,128,256]{3,2,1,0:T(8,128)S(1)}, f32[2,1,128,256]{3,2,1,0:T(8,128)S(1)}, u32[]{:S(2)}, u32[]{:S(2)}) collective-permute-start(f32[2,1,128,256]{3,2,1,0:T(8,128)S(1)} %pad_maximum_fusion.4), channel_id=1, source_target_pairs={{1,0},{2,1},{3,2},{4,3},{5,4},{6,5},{7,6},{8,7},{9,8},{10,9},{11,1... | collective-permute-start | bytes 786440 | tf_op jit(solution)/shard_map/ppermute | solution.py:12
  31.9 6.5 collective-permute-start
  41.3 6.5 collective-permute-start
  50.7 6.5 collective-permute-start
  60.1 6.5 collective-permute-start
  69.5 6.5 collective-permute-start
  78.9 6.5 collective-permute-start
  88.4 6.5 collective-permute-start
  97.8 6.5 collective-permute-start
  107.2 6.5 collective-permute-start
  116.6 6.5 collective-permute-start
  126.0 6.5 collective-permute-start
  135.4 6.5 collective-permute-start
  144.8 6.5 collective-permute-start
  154.3 85.0 %collective-permute-start = (f32[2,128,128]{2,1,0:T(8,128)}, f32[2,128,128]{2,1,0:T(8,128)S(1)}, u32[]{:S(2)}, u32[]{:S(2)}) collective-permute-start(f32[2,128,128]{2,1,0:T(8,128)} %get-tuple-element.1540), channel_id=1, source_target_pairs={{0,32},{32,64},{64,96},{96,128},{128,160},{160,192},{192,224},{224... | collective-permute-start | bytes 393224 | tf_op jit(solution)/shard_map/while/body/eval_jaxpr/ppermute | solution.py:18
  250.0 7.7 collective-permute-start
  268.3 9.4 collective-permute-start
  288.4 13.0 %collective-permute-start = (f32[2,128,128]{2,1,0:T(8,128)}, f32[2,128,128]{2,1,0:T(8,128)S(1)}, u32[]{:S(2)}, u32[]{:S(2)}) collective-permute-start(f32[2,128,128]{2,1,0:T(8,128)} %get-tuple-element.1540), channel_id=1, source_target_pairs={{0,32},{32,64},{64,96},{96,128},{128,160},{160,192},{192,224},{224... | collective-permute-start | bytes 393224 | tf_op jit(solution)/shard_map/while/body/eval_jaxpr/ppermute | solution.py:18
  312.2 13.0 %collective-permute-start = (f32[2,128,128]{2,1,0:T(8,128)}, f32[2,128,128]{2,1,0:T(8,128)S(1)}, u32[]{:S(2)}, u32[]{:S(2)}) collective-permute-start(f32[2,128,128]{2,1,0:T(8,128)} %get-tuple-element.1540), channel_id=1, source_target_pairs={{0,32},{32,64},{64,96},{96,128},{128,160},{160,192},{192,224},{224... | collective-permute-start | bytes 393224 | tf_op jit(solution)/shard_map/while/body/eval_jaxpr/ppermute | solution.py:18
  335.9 13.0 %collective-permute-start = (f32[2,128,128]{2,1,0:T(8,128)}, f32[2,128,128]{2,1,0:T(8,128)S(1)}, u32[]{:S(2)}, u32[]{:S(2)}) collective-permute-start(f32[2,128,128]{2,1,0:T(8,128)} %get-tuple-element.1540), channel_id=1, source_target_pairs={{0,32},{32,64},{64,96},{96,128},{128,160},{160,192},{192,224},{224... | collective-permute-start | bytes 393224 | tf_op jit(solution)/shard_map/while/body/eval_jaxpr/ppermute | solution.py:18
  359.7 13.0 %collective-permute-start = (f32[2,128,128]{2,1,0:T(8,128)}, f32[2,128,128]{2,1,0:T(8,128)S(1)}, u32[]{:S(2)}, u32[]{:S(2)}) collective-permute-start(f32[2,128,128]{2,1,0:T(8,128)} %get-tuple-element.1540), channel_id=1, source_target_pairs={{0,32},{32,64},{64,96},{96,128},{128,160},{160,192},{192,224},{224... | collective-permute-start | bytes 393224 | tf_op jit(solution)/shard_map/while/body/eval_jaxpr/ppermute | solution.py:18
  383.4 13.1 %collective-permute-start = (f32[2,128,128]{2,1,0:T(8,128)}, f32[2,128,128]{2,1,0:T(8,128)S(1)}, u32[]{:S(2)}, u32[]{:S(2)}) collective-permute-start(f32[2,128,128]{2,1,0:T(8,128)} %get-tuple-element.1540), channel_id=1, source_target_pairs={{0,32},{32,64},{64,96},{96,128},{128,160},{160,192},{192,224},{224... | collective-permute-start | bytes 393224 | tf_op jit(solution)/shard_map/while/body/eval_jaxpr/ppermute | solution.py:18
  399.4 20.8 %collective-permute-start = (f32[2,128,128]{2,1,0:T(8,128)}, f32[2,128,128]{2,1,0:T(8,128)S(1)}, u32[]{:S(2)}, u32[]{:S(2)}) collective-permute-start(f32[2,128,128]{2,1,0:T(8,128)} %get-tuple-element.1540), channel_id=1, source_target_pairs={{0,32},{32,64},{64,96},{96,128},{128,160},{160,192},{192,224},{224... | collective-permute-start | bytes 393224 | tf_op jit(solution)/shard_map/while/body/eval_jaxpr/ppermute | solution.py:18
  423.1 6.5 collective-permute-start
  432.5 6.5 collective-permute-start
  441.9 6.5 collective-permute-start
  460.8 6.5 collective-permute-start
  470.2 6.5 collective-permute-start
  479.6 6.5 collective-permute-start
  489.0 6.5 collective-permute-start
  498.4 6.5 collective-permute-start
  507.1 10.2 collective-permute-start.1
  525.7 10.2 collective-permute-start.1
  544.3 10.4 collective-permute-start.1
  563.1 10.4 collective-permute-start.1
  581.9 10.4 collective-permute-start.1
  600.8 10.4 collective-permute-start.1
  619.6 10.4 collective-permute-start.1
  638.4 10.4 collective-permute-start.1
  650.2 13.1 %collective-permute-start.1 = (f32[2,128,128]{2,1,0:T(8,128)S(1)}, f32[2,128,128]{2,1,0:T(8,128)S(1)}, u32[]{:S(2)}, u32[]{:S(2)}) collective-permute-start(f32[2,128,128]{2,1,0:T(8,128)S(1)} %get-tuple-element.1561), channel_id=1, source_target_pairs={{32,0},{64,32},{96,64},{128,96},{160,128},{192,160},{224,192},{256... | collective-permute-start | bytes 393224 | tf_op jit(solution)/shard_map/while/body/eval_jaxpr/ppermute | solution.py:18
  664.8 10.5 collective-permute-start.1
  676.6 10.4 collective-permute-start.1
  688.5 10.4 collective-permute-start.1
  700.2 13.0 %collective-permute-start.1 = (f32[2,128,128]{2,1,0:T(8,128)S(1)}, f32[2,128,128]{2,1,0:T(8,128)S(1)}, u32[]{:S(2)}, u32[]{:S(2)}) collective-permute-start(f32[2,128,128]{2,1,0:T(8,128)S(1)} %get-tuple-element.1561), channel_id=1, source_target_pairs={{32,0},{64,32},{96,64},{128,96},{160,128},{192,160},{224,192},{256... | collective-permute-start | bytes 393224 | tf_op jit(solution)/shard_map/while/body/eval_jaxpr/ppermute | solution.py:18
  714.7 10.3 collective-permute-start.1
  726.3 10.4 collective-permute-start.1
  738.1 10.5 collective-permute-start.1
  750.0 12.7 %collective-permute-start.1 = (f32[2,128,128]{2,1,0:T(8,128)S(1)}, f32[2,128,128]{2,1,0:T(8,128)S(1)}, u32[]{:S(2)}, u32[]{:S(2)}) collective-permute-start(f32[2,128,128]{2,1,0:T(8,128)S(1)} %get-tuple-element.1561), channel_id=1, source_target_pairs={{32,0},{64,32},{96,64},{128,96},{160,128},{192,160},{224,192},{256... | collective-permute-start | bytes 393224 | tf_op jit(solution)/shard_map/while/body/eval_jaxpr/ppermute | solution.py:18
  764.1 10.5 collective-permute-start.1
  776.0 10.2 collective-permute-start.1
  787.6 10.5 collective-permute-start.1
  799.4 13.9 %collective-permute-start.1 = (f32[2,128,128]{2,1,0:T(8,128)S(1)}, f32[2,128,128]{2,1,0:T(8,128)S(1)}, u32[]{:S(2)}, u32[]{:S(2)}) collective-permute-start(f32[2,128,128]{2,1,0:T(8,128)S(1)} %get-tuple-element.1561), channel_id=1, source_target_pairs={{32,0},{64,32},{96,64},{128,96},{160,128},{192,160},{224,192},{256... | collective-permute-start | bytes 393224 | tf_op jit(solution)/shard_map/while/body/eval_jaxpr/ppermute | solution.py:18
  814.7 10.5 collective-permute-start.1
  826.6 10.2 collective-permute-start.1
  838.2 10.5 collective-permute-start.1
  850.1 12.7 %collective-permute-start.1 = (f32[2,128,128]{2,1,0:T(8,128)S(1)}, f32[2,128,128]{2,1,0:T(8,128)S(1)}, u32[]{:S(2)}, u32[]{:S(2)}) collective-permute-start(f32[2,128,128]{2,1,0:T(8,128)S(1)} %get-tuple-element.1561), channel_id=1, source_target_pairs={{32,0},{64,32},{96,64},{128,96},{160,128},{192,160},{224,192},{256... | collective-permute-start | bytes 393224 | tf_op jit(solution)/shard_map/while/body/eval_jaxpr/ppermute | solution.py:18
  864.2 10.5 collective-permute-start.1
  876.1 10.2 collective-permute-start.1
  887.6 10.5 collective-permute-start.1
  899.5 12.7 %collective-permute-start.1 = (f32[2,128,128]{2,1,0:T(8,128)S(1)}, f32[2,128,128]{2,1,0:T(8,128)S(1)}, u32[]{:S(2)}, u32[]{:S(2)}) collective-permute-start(f32[2,128,128]{2,1,0:T(8,128)S(1)} %get-tuple-element.1561), channel_id=1, source_target_pairs={{32,0},{64,32},{96,64},{128,96},{160,128},{192,160},{224,192},{256... | collective-permute-start | bytes 393224 | tf_op jit(solution)/shard_map/while/body/eval_jaxpr/ppermute | solution.py:18
  913.6 10.5 collective-permute-start.1
  925.5 10.2 collective-permute-start.1
  936.7 13.9 %collective-permute-start.3 = (f32[2,1,128,256]{3,2,1,0:T(8,128)S(1)}, f32[2,1,128,256]{3,2,1,0:T(8,128)S(1)}, u32[]{:S(2)}, u32[]{:S(2)}) collective-permute-start(f32[2,1,128,256]{3,2,1,0:T(8,128)S(1)} %slice.101), channel_id=1, source_target_pairs={{31,0},{0,1},{1,2},{2,3},{3,4},{4,5},{5,6},{6,7},{7,8},{8,9},{9,10... | collective-permute-start | bytes 786440 | tf_op jit(solution)/shard_map/ppermute | solution.py:12
  (7 other events, 85.6 us)
Sparse Core Ops, SparseCore 0:
  938.8 229.1 reduce-scatter.1
where the time goes:
time: 1270 us; the launch traced here: 1250 us
  waiting for transfers between devices  363 us (29%)
  local copies, waits for them, and re-layouts  218 us (17%)
  loops' own time  213 us (17%)
  starting transfers between devices  211 us (17%)
  other arithmetic  116 us (9%)
  blocking collectives  77.4 us (6%)
  matrix products  40.2 us (3%)
  between operations  14.2 us (1%)
    reduce_scatter x1, waiting for transfers between devices, per_device(): lax.psum_scatter(tile_total, 'cuts', scatter_dimension=1, tiled=True)  216 us
    ppermute x62, starting transfers between devices, passed_along_2(): lax.ppermute(value, axis, [(source, source + steps) for source in range(f...  195 us
    another operation x1, loops' own time, per_device(): lax.fori_loop(0, step_count, backward, (zero_wave, jnp.zeros_like(object_...  138 us
    ppermute x62, waiting for transfers between devices, passed_along_2(): lax.ppermute(value, axis, [(source, source + steps) for source in range(f...  133 us
    dynamic_update_slice x31, local copies, waits for them, and re-layouts, add_patches(): lax.dynamic_update_slice(gradients, region + jnp.swapaxes(patch_grads, 0,...  108 us
    psum x1, blocking collectives, per_device(): tile_total = lax.psum(probe_sum, 'tile')  77.4 us
    dot_general x116, matrix products, mat_product(): jnp.dot(left_side, right_side, precision=lax.Precision.HIGHEST, preferred...  40.2 us
    broadcast_in_dim x81, local copies, waits for them, and re-layouts, per_device(): zero_wave = jnp.zeros_like(probe)  36.7 us
  transfers between devices with their start and end apart: 65, of which 27 were waited for; matrix products, arithmetic and copies ran while one was open for 18% of the time, Pallas kernels for 0%

commit v1 on v0

v1 whole, which is shorter than its diff:
```python
import functools
import math

import jax
import jax.numpy as jnp
import numpy as np
from jax import lax
from jax.experimental import pallas as pl
from jax.experimental.pallas import tpu as pltpu
from jax.sharding import PartitionSpec as P

VMEM = pltpu.VMEM
SMEM = pltpu.SMEM


def split_bf16(value):
    high = value.astype(jnp.bfloat16)
    low = (value - high.astype(jnp.float32)).astype(jnp.bfloat16)
    return high, low


def exact_dot(left, right):
    return jnp.dot(left, right, precision=lax.Precision.HIGHEST, preferred_element_type=jnp.float32)


def fourier_pair(size):
    places = np.arange(size)
    angle = (places[:, None] * places[None, :] % size) * (2.0 * math.pi / size)
    scale = 1.0 / math.sqrt(size)
    return (np.cos(angle) * scale).astype(np.float32), (-np.sin(angle) * scale).astype(np.float32)


def right_operator(real, imag):
    return jnp.concatenate(
        [jnp.concatenate([real, imag], axis=1), jnp.concatenate([-imag, real], axis=1)], axis=0
    )


def left_operator(real, imag):
    return jnp.concatenate(
        [jnp.concatenate([real, -imag], axis=1), jnp.concatenate([imag, real], axis=1)], axis=0
    )


def rounded_split(matrix):
    high = lax.reduce_precision(matrix, 8, 7)
    return high.astype(jnp.bfloat16), (matrix - high).astype(jnp.bfloat16)


def stacked_right(matrix):
    high, low = rounded_split(matrix)
    return jnp.concatenate([high, high, low], axis=0)


def stacked_left(matrix):
    high, low = rounded_split(matrix)
    return jnp.concatenate([high, high, low], axis=1)


def build_operators(prop_phase):
    size = prop_phase.shape[0]
    f_real, f_imag = fourier_pair(size)
    k_real = jnp.cos(prop_phase)[None, :]
    k_imag = jnp.sin(prop_phase)[None, :]
    l_real = f_real * k_real + f_imag * k_imag
    l_imag = f_real * k_imag - f_imag * k_real
    s_real = exact_dot(l_real, f_real) - exact_dot(l_imag, f_imag)
    s_imag = exact_dot(l_real, f_imag) + exact_dot(l_imag, f_real)
    rights = jnp.stack(
        [
            stacked_right(right_operator(s_real.T, s_imag.T)),
            stacked_right(right_operator(f_real, f_imag)),
            stacked_right(right_operator(f_real, -f_imag)),
            stacked_right(right_operator(s_real, -s_imag)),
        ]
    )
    lefts = jnp.stack(
        [
            stacked_left(left_operator(s_real, s_imag)),
            stacked_left(left_operator(f_real, f_imag)),
            stacked_left(left_operator(f_real, -f_imag)),
            stacked_left(left_operator(s_real.T, -s_imag.T)),
        ]
    )
    return rights, lefts


def sandwich(wide, right, left, size):
    high, low = split_bf16(wide)
    middle = jnp.dot(
        jnp.concatenate([high, low, high], axis=1), right, preferred_element_type=jnp.float32
    )
    tall = jnp.concatenate([middle[:, :size], middle[:, size:]], axis=0)
    high, low = split_bf16(tall)
    out = jnp.dot(
        left, jnp.concatenate([high, low, high], axis=0), preferred_element_type=jnp.float32
    )
    return out[:size], out[size:]


def chain_kernel(live_ref, probe_ref, right_ref, left_ref, window_ref, measured_ref, out_ref, waves):
    slices = window_ref.shape[0]
    size = probe_ref.shape[1]
    extra = size // slices
    live = live_ref[0] > 0

    @pl.when(jnp.logical_not(live))
    def _():
        out_ref[...] = jnp.zeros_like(out_ref)

    @pl.when(live)
    def _():
        def modulated(s, real, imag):
            waves[s, :size, :] = real
            waves[s, size:, :] = imag
            p_real = window_ref[s, :size, :]
            p_imag = window_ref[s, size:, :]
            return jnp.concatenate(
                [real * p_real - imag * p_imag, real * p_imag + imag * p_real], axis=1
            )

        def forward(s, state):
            return sandwich(modulated(s, *state), right_ref[0], left_ref[0], size)

        state = lax.fori_loop(0, slices - 1, forward, (probe_ref[0], probe_ref[1]))
        wide = modulated(slices - 1, *state)
        far_r, far_i = sandwich(wide, right_ref[1], left_ref[1], size)
        excess = 2.0 * (far_r * far_r + far_i * far_i - measured_ref[0])
        wide = jnp.concatenate([excess * far_r, excess * far_i], axis=1)
        inner = sandwich(wide, right_ref[2], left_ref[2], size)

        def deposit(s, h_r, h_i):
            w_r = waves[s, :size, :]
            w_i = waves[s, size:, :]
            p_real = window_ref[s, :size, :]
            p_imag = window_ref[s, size:, :]
            out_ref[s, :size, :] = w_r * h_r + w_i * h_i
            out_ref[s, size : 2 * size, :] = w_r * h_i - w_i * h_r
            return p_real * h_r + p_imag * h_i, p_real * h_i - p_imag * h_r

        def backward(k, state):
            g_r, g_i = deposit(slices - 1 - k, *state)
            return sandwich(
                jnp.concatenate([g_r, g_i], axis=1), right_ref[3], left_ref[3], size
            )

        inner = lax.fori_loop(0, slices - 1, backward, inner)
        g_r, g_i = deposit(0, *inner)
        for s in range(slices):
            out_ref[s, 2 * size : 2 * size + extra, :] = g_r[s * extra : (s + 1) * extra]
            out_ref[s, 2 * size + extra :, :] = g_i[s * extra : (s + 1) * extra]


def run_chain(live, probe, rights, lefts, windows, measured):
    slices, _, size = windows.shape
    rows = 2 * size + 2 * (size // slices)
    vmem = pl.BlockSpec(memory_space=VMEM)
    return pl.pallas_call(
        chain_kernel,
        out_shape=jax.ShapeDtypeStruct((slices, rows, size), jnp.float32),
        in_specs=[pl.BlockSpec(memory_space=SMEM)] + [vmem] * 5,
        out_specs=vmem,
        scratch_shapes=[VMEM((slices, 2 * size, size), jnp.float32)],
        compiler_params=pltpu.CompilerParams(vmem_limit_bytes=40 * 2**20),
        name="chain",
    )(live, probe, rights, lefts, windows, measured)


def cut_kernel(offset_ref, real_ref, imag_ref, below_ref, out_ref, region):
    slots = out_ref.shape[0]
    size = out_ref.shape[2]
    rows = real_ref.shape[1]
    for half in range(2):
        cols = pl.ds(half * size, size)
        region[0, half, :rows, :] = real_ref[0, :, cols]
        region[1, half, :rows, :] = imag_ref[0, :, cols]
        region[0, half, rows:, :] = below_ref[0, :, cols]
        region[1, half, rows:, :] = below_ref[1, :, cols]
    lane = lax.broadcasted_iota(jnp.int32, (size, size), 1)

    def one_slot(n, carry):
        row = offset_ref[n, 0]
        col = offset_ref[n, 1]
        shift = lax.rem(size - col + size, size)
        from_first = lane < size - col
        for part in range(2):
            first = pltpu.roll(region[part, 0, pl.ds(row, size), :], shift, 1)
            second = pltpu.roll(region[part, 1, pl.ds(row, size), :], shift, 1)
            out_ref[n, part * size : (part + 1) * size, :] = jnp.where(from_first, first, second)
        return carry

    lax.fori_loop(0, slots, one_slot, 0)


def cut_windows(offsets, obj_real, obj_imag, below, size):
    slots = offsets.shape[0]
    rows, width = obj_real.shape[1:]
    vmem = pl.BlockSpec(memory_space=VMEM)
    return pl.pallas_call(
        cut_kernel,
        out_shape=jax.ShapeDtypeStruct((slots, 2 * size, size), jnp.float32),
        in_specs=[pl.BlockSpec(memory_space=SMEM)] + [vmem] * 3,
        out_specs=vmem,
        scratch_shapes=[VMEM((2, 2, rows + size, size), jnp.float32)],
        compiler_params=pltpu.CompilerParams(vmem_limit_bytes=24 * 2**20),
        name="cut",
    )(offsets, obj_real, obj_imag, below)


def gather_kernel(offset_ref, terms_ref, own_ref, band_ref, probe_ref, region):
    slots, tall, size = terms_ref.shape
    rows = own_ref.shape[1]
    extra = (tall - 2 * size) // 2
    region[...] = jnp.zeros_like(region)
    lane = lax.broadcasted_iota(jnp.int32, (size, size), 1)

    def one_slot(n, total):
        here = pl.ds(offset_ref[n, 0], size)
        col = offset_ref[n, 1]
        in_first = lane >= col
        for part in range(2):
            term = terms_ref[n, part * size : (part + 1) * size, :]
            turned = pltpu.roll(term, lax.rem(col, size), 1)
            region[part, 0, here, :] = region[part, 0, here, :] + jnp.where(in_first, turned, 0.0)
            region[part, 1, here, :] = region[part, 1, here, :] + jnp.where(in_first, 0.0, turned)
        return total + terms_ref[n, 2 * size :, :]

    total = lax.fori_loop(0, slots, one_slot, jnp.zeros((2 * extra, size), jnp.float32))
    for half in range(2):
        cols = pl.ds(half * size, size)
        own_ref[:, :, cols] = region[:, half, :rows, :]
        band_ref[:, :, cols] = region[:, half, rows:, :]
    probe_ref[...] = total


def add_windows(offsets, terms, rows, width):
    slots, tall, size = terms.shape
    vmem = pl.BlockSpec(memory_space=VMEM)
    return pl.pallas_call(
        gather_kernel,
        out_shape=[
            jax.ShapeDtypeStruct((2, rows, width), jnp.float32),
            jax.ShapeDtypeStruct((2, size, width), jnp.float32),
            jax.ShapeDtypeStruct((tall - 2 * size, size), jnp.float32),
        ],
        in_specs=[pl.BlockSpec(memory_space=SMEM), vmem],
        out_specs=[vmem] * 3,
        scratch_shapes=[VMEM((2, 2, rows + size, size), jnp.float32)],
        compiler_params=pltpu.CompilerParams(vmem_limit_bytes=24 * 2**20),
        name="gather",
    )(offsets, terms)


def passed_along(block, axis, distance):
    count = lax.axis_size(axis)
    return lax.ppermute(block, axis, [((i - distance) % count, i) for i in range(count)])


def per_device(obj_real, obj_imag, probe_real, probe_imag, prop_phase, intensity, offsets, counts):
    size = probe_real.shape[0]
    rows, width = obj_real.shape[1:]
    slot = lax.axis_index("cuts")
    below = passed_along(jnp.concatenate([obj_real, obj_imag]), "tile", -1)
    rights, lefts = build_operators(prop_phase)
    probe = jnp.stack([probe_real, probe_imag])
    measured = lax.dynamic_slice_in_dim(intensity, slot, 1, 0)
    live = (slot < counts).astype(jnp.int32)
    windows = cut_windows(offsets, obj_real, obj_imag, below, size)
    windows = lax.all_to_all(windows, "cuts", 0, 0, tiled=True)
    terms = run_chain(live, probe, rights, lefts, windows, measured)
    terms = lax.all_to_all(terms, "cuts", 0, 0, tiled=True)
    own, band, probe_part = add_windows(offsets, terms, rows, width)
    band = passed_along(band, "tile", 1)
    tiles = lax.axis_size("tile")
    spread = jnp.broadcast_to(probe_part[None], (tiles,) + probe_part.shape)
    probe_parts = lax.all_to_all(spread, "tile", 0, 0, tiled=True)
    probe_grad = jnp.sum(probe_parts, axis=0).reshape(2, -1, size)
    object_grad = (own + band)[:, None]
    return object_grad, probe_grad


def solution(mesh):
    in_specs = (
        P("cuts", "tile", None),
        P("cuts", "tile", None),
        P(),
        P(),
        P(),
        P("tile", None, None),
        P("tile", None),
        P("tile"),
    )
    out_specs = (P(None, "cuts", "tile", None), P(None, "cuts", None))
    return jax.shard_map(
        per_device, mesh=mesh, in_specs=in_specs, out_specs=out_specs, check_vma=False
    )
```

time: 1270 us -> 191 us (0.15)
  the two profiles are of different devices: /device:TPU:56 before, /device:TPU:1 now
where the time goes in v1:
time: 191 us; the launch traced here: 190 us
  blocking collectives  74.1 us (39%)
  waiting for transfers between devices  56.9 us (30%)
  starting transfers between devices  32.8 us (17%)
  other arithmetic  9.07 us (5%)
  local copies, waits for them, and re-layouts  7.26 us (4%)
  Pallas kernels  6.84 us (4%)
    all_to_all x1, blocking collectives, per_device(): terms = lax.all_to_all(terms, 'cuts', 0, 0, tiled=True)  74.1 us
    all_to_all x1, waiting for transfers between devices, per_device(): windows = lax.all_to_all(windows, 'cuts', 0, 0, tiled=True)  38.9 us
    ppermute x2, waiting for transfers between devices, passed_along(): lax.ppermute(block, axis, [((i - distance) % count, i) for i in range(cou...  18 us
    ppermute x2, starting transfers between devices, passed_along(): lax.ppermute(block, axis, [((i - distance) % count, i) for i in range(cou...  16.8 us
    all_to_all x1, starting transfers between devices, per_device(): windows = lax.all_to_all(windows, 'cuts', 0, 0, tiled=True)  8.79 us
    all_to_all x1, starting transfers between devices, per_device(): probe_parts = lax.all_to_all(spread, 'tile', 0, 0, tiled=True)  7.19 us
    unnamed x31, local copies, waits for them, and re-layouts  5.62 us
    pallas_call x1, Pallas kernels, cut_windows(): pl.pallas_call(cut_kernel, out_shape=jax.ShapeDtypeStruct((slots, 2 * siz...  4.24 us
  transfers between devices with their start and end apart: 4, of which 3 were waited for; matrix products, arithmetic and copies ran while one was open for 6% of the time, Pallas kernels for 0%

profile of v1, /device:TPU:1, one launch (start us, length us, event | category | flops | bytes accessed | tf_op | source)
XLA Modules:
  0.0 190.0 jit_solution(5835452631818090665)
XLA Ops:
  0.6 0.0 copy-start
  0.6 1.1 pad_maximum_fusion.2
  1.7 13.7 %collective-permute-start = (f32[2,128,256]{2,1,0:T(8,128)S(1)}, f32[2,128,256]{2,1,0:T(8,128)S(1)}, u32[]{:S(2)}, u32[]{:S(2)}) collective-permute-start(f32[2,128,256]{2,1,0:T(8,128)S(1)} %pad_maximum_fusion.2), channel_id=1, source_target_pairs={{1,0},{2,1},{3,2},{4,3},{5,4},{6,5},{7,6},{8,7},{9,8},{10,9},{11,1... | collective-permute-start | bytes 786440 | tf_op jit(solution)/shard_map/ppermute | solution.py:256
  15.4 0.8 copy.42.offset_ref
  16.2 4.2 %collective-permute-done.below_ref = f32[2,128,256]{2,1,0:T(8,128)S(1)} collective-permute-done((f32[2,128,256]{2,1,0:T(8,128)S(1)}, f32[2,128,256]{2,1,0:T(8,128)S(1)}, u32[]{:S(2)}, u32[]{:S(2)}) %collective-permute-start) | collective-permute-done | bytes 262176 | tf_op jit(solution)/shard_map/ppermute | solution.py:256
  20.4 0.0 copy-start.3
  20.4 0.9 copy-done.3
  21.3 0.0 copy-start.4
  21.3 0.9 copy-done.4
  22.2 4.2 %cut.1 = f32[16,256,128]{2,1,0:T(8,128)} custom-call(s32[16,2]{1,0:T(8,128)S(1)} %copy.42.offset_ref, f32[1,128,256]{2,1,0:T(8,128)S(1)} %copy-done.3, f32[1,128,256]{2,1,0:T(8,128)S(1)} %copy-done.4, f32[2,128,256]{2,1,0:T(8,128)S(1)} %collective-permute-done.below_ref), custom_call_target="tpu_custom_call" | custom-call | tf_op jit(solution)/shard_map/cut/pallas_call | solution.py:199
  26.4 0.0 copy-start.14
  26.4 0.0 copy-start.5
  26.4 0.0 copy-start.6
  26.4 8.8 %all-to-all-start = ((f32[16,256,128]{2,1,0:T(8,128)}), f32[16,256,128]{2,1,0:T(8,128)S(1)}, u32[]{:S(2)}, u32[]{:S(2)}) async-start(f32[16,256,128]{2,1,0:T(8,128)} %cut.1), calls=%async_computation | async-start | bytes 4194304 | tf_op jit(solution)/shard_map/all_to_all | solution.py:269
  35.9 0.0 copy-done.14
  35.9 0.0 copy-done.5
  35.9 0.0 copy-done.6
  36.0 0.2 fusion.1
  36.2 0.8 fusion.12
  37.0 0.0 copy-start.9
  37.0 0.2 fusion.2
  37.2 0.2 convolution_subtract_fusion
  37.5 0.0 copy-start.8
  37.5 0.2 copy-done.9
  37.7 0.1 copy.36
  37.8 0.9 reduce-precision_convert_fusion.1
  38.6 0.8 copy.37
  39.4 0.0 copy-done.8
  39.4 0.0 copy-done
  39.4 0.0 copy-start.7
  39.4 0.9 pad_maximum_fusion.3.probe_ref
  40.3 0.0 copy-start.12
  40.3 0.0 copy-start.13
  40.4 1.0 reduce-precision_convert_fusion
  41.4 1.0 maximum_bitcast_fusion.2
  42.4 0.0 copy-done.7
  42.4 0.1 maximum_bitcast_fusion
  42.5 0.0 copy-done.12
  42.5 0.0 copy-done.13
  42.5 0.0 copy-start.10
  42.5 0.0 copy-start.11
  42.5 1.3 pad_maximum_fusion.right_ref
  43.9 0.0 copy-done.10
  43.9 0.0 copy-done.11
  43.9 1.4 pad_maximum_fusion.1.left_ref
  45.3 38.9 %all-to-all-done.window_ref = f32[16,256,128]{2,1,0:T(8,128)S(1)} async-done(((f32[16,256,128]{2,1,0:T(8,128)}), f32[16,256,128]{2,1,0:T(8,128)S(1)}, u32[]{:S(2)}, u32[]{:S(2)}) %all-to-all-start) | async-done | bytes 2097184 | tf_op jit(solution)/shard_map/all_to_all | solution.py:269
  84.2 0.0 copy-start.1
  84.2 1.4 copy-done.1
  85.6 0.0 copy-start.2
  85.6 1.4 copy-done.2
  87.0 0.1 chain.1
  87.1 74.1 %all_to_all.15.terms_ref = f32[16,272,128]{2,1,0:T(8,128)S(1)} all-to-all(f32[16,272,128]{2,1,0:T(8,128)S(1)} %chain.1), channel_id=1, replica_groups=mesh['cuts'=16,'tile'=32] {'cuts'}, dimensions={0} | all-to-all | bytes 4456448 | tf_op jit(solution)/shard_map/all_to_all | solution.py:271
  161.3 2.5 %gather.1 = (f32[2,128,256]{2,1,0:T(8,128)S(1)}, f32[2,128,256]{2,1,0:T(8,128)S(1)}, f32[16,128]{1,0:T(8,128)S(1)}) custom-call(s32[16,2]{1,0:T(8,128)S(1)} %copy.42.offset_ref, f32[16,272,128]{2,1,0:T(8,128)S(1)} %all_to_all.15.terms_ref), custom_call_target="tpu_custom_call" | custom-call | tf_op jit(solution)/shard_map/gather/pallas_call | solution.py:239
  163.7 0.7 broadcast_in_dim.5
  164.5 7.2 %all-to-all-start.2 = ((f32[32,16,128]{2,1,0:T(8,128)}), f32[32,16,128]{2,1,0:T(8,128)S(1)}, u32[]{:S(2)}, u32[]{:S(2)}) async-start(f32[32,16,128]{2,1,0:T(8,128)} %broadcast_in_dim.5), calls=%async_computation.2 | async-start | bytes 524288 | tf_op jit(solution)/shard_map/all_to_all | solution.py:276
  171.7 3.1 %collective-permute-start.1 = (f32[2,128,256]{2,1,0:T(8,128)S(1)}, f32[2,128,256]{2,1,0:T(8,128)S(1)}, u32[]{:S(2)}, u32[]{:S(2)}) collective-permute-start(f32[2,128,256]{2,1,0:T(8,128)S(1)} %get-tuple-element.6), channel_id=1, source_target_pairs={{31,0},{0,1},{1,2},{2,3},{3,4},{4,5},{5,6},{6,7},{7,8},{8,9},{9,10... | collective-permute-start | bytes 786440 | tf_op jit(solution)/shard_map/ppermute | solution.py:256
  174.8 13.8 %collective-permute-done.1 = f32[2,128,256]{2,1,0:T(8,128)S(1)} collective-permute-done((f32[2,128,256]{2,1,0:T(8,128)S(1)}, f32[2,128,256]{2,1,0:T(8,128)S(1)}, u32[]{:S(2)}, u32[]{:S(2)}) %collective-permute-start.1) | collective-permute-done | bytes 262176 | tf_op jit(solution)/shard_map/ppermute | solution.py:256
  188.6 0.7 add_bitcast_fusion
  189.3 0.0 all-to-all-done.2
  189.3 0.6 reduce_sum.9
  (4 shorter events, 0.1 us)
Async XLA Ops:
  0.6 38.8 %copy-start = (f32[16,128,128]{2,1,0:T(8,128)S(1)}, f32[16,128,128]{2,1,0:T(8,128)}, u32[]{:S(2)}) copy-start(f32[16,128,128]{2,1,0:T(8,128)} %param.31) | copy-start | bytes 3145732
  1.7 18.7 %collective-permute-start = (f32[2,128,256]{2,1,0:T(8,128)S(1)}, f32[2,128,256]{2,1,0:T(8,128)S(1)}, u32[]{:S(2)}, u32[]{:S(2)}) collective-permute-start(f32[2,128,256]{2,1,0:T(8,128)S(1)} %pad_maximum_fusion.2), channel_id=1, source_target_pairs={{1,0},{2,1},{3,2},{4,3},{5,4},{6,5},{7,6},{8,7},{9,8},{10,9},{11,1... | collective-permute-start | bytes 786440 | tf_op jit(solution)/shard_map/ppermute | solution.py:256
  20.4 0.9 copy-start.3
  21.3 0.9 copy-start.4
  26.4 9.5 %copy-start.14 = (f32[128]{0:T(128)S(1)}, f32[128]{0:T(128)}, u32[]{:S(2)}) copy-start(f32[128]{0:T(128)} %param.30) | copy-start | bytes 1540
  26.4 9.5 %copy-start.5 = (f32[128,128]{1,0:T(8,128)S(1)}, f32[128,128]{1,0:T(8,128)}, u32[]{:S(2)}) copy-start(f32[128,128]{1,0:T(8,128)} %constant.18.clone) | copy-start | bytes 196612
  26.4 9.5 %copy-start.6 = (f32[128,128]{1,0:T(8,128)S(1)}, f32[128,128]{1,0:T(8,128)}, u32[]{:S(2)}) copy-start(f32[128,128]{1,0:T(8,128)} %constant.19.clone) | copy-start | bytes 196612
  26.4 57.7 %all-to-all-start = ((f32[16,256,128]{2,1,0:T(8,128)}), f32[16,256,128]{2,1,0:T(8,128)S(1)}, u32[]{:S(2)}, u32[]{:S(2)}) async-start(f32[16,256,128]{2,1,0:T(8,128)} %cut.1), calls=%async_computation | async-start | bytes 4194304 | tf_op jit(solution)/shard_map/all_to_all | solution.py:269
  37.0 0.6 copy-start.9
  37.5 1.9 %copy-start.8 = (f32[128,128]{1,0:T(8,128)}, f32[128,128]{1,0:T(8,128)S(1)}, u32[]{:S(2)}) copy-start(f32[128,128]{1,0:T(8,128)S(1)} %convolution_subtract_fusion) | copy-start | bytes 196612
  39.4 3.0 %copy-start.7 = (bf16[256,256]{1,0:T(8,128)(2,1)S(1)}, bf16[256,256]{1,0:T(8,128)(2,1)}, u32[]{:S(2)}) copy-start(bf16[256,256]{1,0:T(8,128)(2,1)} %copy.37) | copy-start | bytes 393220
  40.3 2.1 %copy-start.12 = (bf16[1,768,256]{2,1,0:T(8,128)(2,1)S(1)}, bf16[1,768,256]{2,1,0:T(8,128)(2,1)}, u32[]{:S(2)}) copy-start(bf16[1,768,256]{2,1,0:T(8,128)(2,1)} %constant.43) | copy-start | bytes 1179652
  40.3 2.1 %copy-start.13 = (bf16[1,768,256]{2,1,0:T(8,128)(2,1)S(1)}, bf16[1,768,256]{2,1,0:T(8,128)(2,1)}, u32[]{:S(2)}) copy-start(bf16[1,768,256]{2,1,0:T(8,128)(2,1)} %constant.34) | copy-start | bytes 1179652
  42.5 1.4 copy-start.10
  42.5 1.4 copy-start.11
  84.2 1.4 copy-start.1
  85.6 1.4 copy-start.2
  164.5 24.9 %all-to-all-start.2 = ((f32[32,16,128]{2,1,0:T(8,128)}), f32[32,16,128]{2,1,0:T(8,128)S(1)}, u32[]{:S(2)}, u32[]{:S(2)}) async-start(f32[32,16,128]{2,1,0:T(8,128)} %broadcast_in_dim.5), calls=%async_computation.2 | async-start | bytes 524288 | tf_op jit(solution)/shard_map/all_to_all | solution.py:276
  171.7 16.9 %collective-permute-start.1 = (f32[2,128,256]{2,1,0:T(8,128)S(1)}, f32[2,128,256]{2,1,0:T(8,128)S(1)}, u32[]{:S(2)}, u32[]{:S(2)}) collective-permute-start(f32[2,128,256]{2,1,0:T(8,128)S(1)} %get-tuple-element.6), channel_id=1, source_target_pairs={{31,0},{0,1},{1,2},{2,3},{3,4},{4,5},{5,6},{6,7},{7,8},{8,9},{9,10... | collective-permute-start | bytes 786440 | tf_op jit(solution)/shard_map/ppermute | solution.py:256

commit v2 on v1

v2 whole, which is shorter than its diff:
```python
import functools
import math

import jax
import jax.numpy as jnp
import numpy as np
from jax import lax
from jax.experimental import pallas as pl
from jax.experimental.pallas import tpu as pltpu
from jax.sharding import PartitionSpec as P

VMEM = pltpu.VMEM
SMEM = pltpu.SMEM


def split_bf16(value):
    high = value.astype(jnp.bfloat16)
    low = (value - high.astype(jnp.float32)).astype(jnp.bfloat16)
    return high, low


def exact_dot(left, right):
    return jnp.dot(left, right, precision=lax.Precision.HIGHEST, preferred_element_type=jnp.float32)


def fourier_pair(size):
    places = np.arange(size)
    angle = (places[:, None] * places[None, :] % size) * (2.0 * math.pi / size)
    scale = 1.0 / math.sqrt(size)
    return (np.cos(angle) * scale).astype(np.float32), (-np.sin(angle) * scale).astype(np.float32)


def rounded_split(matrix, seed):
    high = lax.reduce_precision(matrix, 8, 7)
    dither = np.random.default_rng(seed).uniform(-1.0, 1.0, matrix.shape) * 0.003
    low = (matrix - high) * (1.0 + dither).astype(np.float32)
    return high.astype(jnp.bfloat16), low.astype(jnp.bfloat16)


def build_matrices(prop_phase):
    size = prop_phase.shape[0]
    f_real, f_imag = fourier_pair(size)
    k_real = jnp.cos(prop_phase)[None, :]
    k_imag = jnp.sin(prop_phase)[None, :]
    l_real = f_real * k_real + f_imag * k_imag
    l_imag = f_real * k_imag - f_imag * k_real
    s_real = exact_dot(l_real, f_real) - exact_dot(l_imag, f_imag)
    s_imag = exact_dot(l_real, f_imag) + exact_dot(l_imag, f_real)
    return rounded_split(jnp.stack([s_real, s_imag, s_real.T, s_imag.T, f_real, f_imag]), 1)


def assemble(matrix_ref, right_ref, left_ref):
    size = matrix_ref.shape[1]
    uses = ((0, 2, 1.0), (4, 4, 1.0), (4, 4, -1.0), (2, 0, -1.0))
    for which, (left, right, sign) in enumerate(uses):
        real, imag = matrix_ref[right], matrix_ref[right + 1] * sign
        right_ref[which, :size, :size] = real
        right_ref[which, :size, size:] = imag
        right_ref[which, size:, :size] = -imag
        right_ref[which, size:, size:] = real
        left_ref[which, :, :size] = matrix_ref[left]
        left_ref[which, :, size:] = matrix_ref[left + 1] * sign


def sandwich(wide, operators, which):
    dot = functools.partial(jnp.dot, preferred_element_type=jnp.float32)
    right_high, right_low, left_high, left_low = (ref[which] for ref in operators)
    size = wide.shape[0]
    high, low = split_bf16(wide)
    middle = dot(high, right_high) + dot(low, right_high) + dot(high, right_low)
    swapped = jnp.concatenate([-middle[:, size:], middle[:, :size]], axis=1)
    high, low = split_bf16(jnp.concatenate([middle, swapped], axis=0))
    out = dot(left_high, high) + dot(left_low, high) + dot(left_high, low)
    return out[:, :size], out[:, size:]


def chain_kernel(live_ref, probe_ref, *refs):
    high_ref, low_ref, measured_ref, window_ref, out_ref, waves, *operators = refs
    slices = window_ref.shape[0]
    size = probe_ref.shape[1]
    extra = size // slices
    live = live_ref[0] > 0

    @pl.when(jnp.logical_not(live))
    def _():
        out_ref[...] = jnp.zeros_like(out_ref)

    @pl.when(live)
    def _():
        assemble(high_ref, operators[0], operators[2])
        assemble(low_ref, operators[1], operators[3])

        def modulated(s, real, imag):
            waves[s, :size, :] = real
            waves[s, size:, :] = imag
            p_real = window_ref[s, :size, :]
            p_imag = window_ref[s, size:, :]
            return jnp.concatenate(
                [real * p_real - imag * p_imag, real * p_imag + imag * p_real], axis=1
            )

        state = (probe_ref[0], probe_ref[1])
        for s in range(slices - 1):
            state = sandwich(modulated(s, *state), operators, 0)
        wide = modulated(slices - 1, *state)
        far_r, far_i = sandwich(wide, operators, 1)
        excess = 2.0 * (far_r * far_r + far_i * far_i - measured_ref[0])
        wide = jnp.concatenate([excess * far_r, excess * far_i], axis=1)
        h_r, h_i = sandwich(wide, operators, 2)
        for s in reversed(range(slices)):
            w_r = waves[s, :size, :]
            w_i = waves[s, size:, :]
            p_real = window_ref[s, :size, :]
            p_imag = window_ref[s, size:, :]
            out_ref[s, :size, :] = w_r * h_r + w_i * h_i
            out_ref[s, size : 2 * size, :] = w_r * h_i - w_i * h_r
            g_r = p_real * h_r + p_imag * h_i
            g_i = p_real * h_i - p_imag * h_r
            if s > 0:
                wide = jnp.concatenate([g_r, g_i], axis=1)
                h_r, h_i = sandwich(wide, operators, 3)
        for s in range(slices):
            out_ref[s, 2 * size : 2 * size + extra, :] = g_r[s * extra : (s + 1) * extra]
            out_ref[s, 2 * size + extra :, :] = g_i[s * extra : (s + 1) * extra]


def run_chain(live, probe, matrices, windows, measured):
    slices, _, size = windows.shape
    rows = 2 * size + 2 * (size // slices)
    vmem = pl.BlockSpec(memory_space=VMEM)
    return pl.pallas_call(
        chain_kernel,
        out_shape=jax.ShapeDtypeStruct((slices, rows, size), jnp.float32),
        in_specs=[pl.BlockSpec(memory_space=SMEM)] + [vmem] * 5,
        out_specs=vmem,
        scratch_shapes=[
            VMEM((slices, 2 * size, size), jnp.float32),
            VMEM((4, 2 * size, 2 * size), jnp.bfloat16),
            VMEM((4, 2 * size, 2 * size), jnp.bfloat16),
            VMEM((4, size, 2 * size), jnp.bfloat16),
            VMEM((4, size, 2 * size), jnp.bfloat16),
        ],
        compiler_params=pltpu.CompilerParams(vmem_limit_bytes=16 * 2**20),
        name="chain",
    )(live, probe, *matrices, measured, windows)


def cut_kernel(
    offset_ref, real_hbm, imag_hbm, real_below, imag_below, out_hbm, region, out_ref, sems, out_sems
):
    slots, _, size = out_ref.shape
    rows = real_hbm.shape[1]
    parts = ((0, 0, real_hbm), (1, 0, imag_hbm), (0, rows, real_below), (1, rows, imag_below))
    arrivals = []
    for part, first, source in parts:
        for half in range(2):
            arrivals.append(
                pltpu.make_async_copy(
                    source.at[0, :, pl.ds(half * size, size)],
                    region.at[part, half, pl.ds(first, rows)],
                    sems.at[len(arrivals)],
                )
            )
    for arrival in arrivals:
        arrival.start()
    for arrival in arrivals:
        arrival.wait()
    lane = lax.broadcasted_iota(jnp.int32, (size, size), 1)

    def one_slot(n, carry):
        here = pl.ds(offset_ref[n, 0], size)
        col = offset_ref[n, 1]
        shift = lax.rem(size - col + size, size)
        in_first = lane >= col
        for part in range(2):
            mixed = jnp.where(in_first, region[part, 0, here, :], region[part, 1, here, :])
            out_ref[n, part * size : (part + 1) * size, :] = pltpu.roll(mixed, shift, 1)
        pltpu.make_async_copy(out_ref.at[n], out_hbm.at[n], out_sems.at[n]).start()
        return carry

    lax.fori_loop(0, slots, one_slot, 0, unroll=2)
    for n in range(slots):
        pltpu.make_async_copy(out_ref.at[n], out_hbm.at[n], out_sems.at[n]).wait()


def cut_windows(offsets, obj_real, obj_imag, below_real, below_imag, size):
    slots = offsets.shape[0]
    _, rows, width = obj_real.shape
    return pl.pallas_call(
        cut_kernel,
        out_shape=jax.ShapeDtypeStruct((slots, 2 * size, size), jnp.float32),
        in_specs=[pl.BlockSpec(memory_space=SMEM)] + [pl.BlockSpec(memory_space=pl.ANY)] * 4,
        out_specs=pl.BlockSpec(memory_space=pl.ANY),
        scratch_shapes=[
            VMEM((2, 2, 2 * rows, size), jnp.float32),
            VMEM((slots, 2 * size, size), jnp.float32),
            pltpu.SemaphoreType.DMA((8,)),
            pltpu.SemaphoreType.DMA((slots,)),
        ],
        compiler_params=pltpu.CompilerParams(vmem_limit_bytes=60 * 2**20),
        name="cut",
    )(offsets, obj_real, obj_imag, below_real, below_imag)


def gather_kernel(offset_ref, terms_ref, own_ref, band_ref, region):
    slots, _, size = terms_ref.shape
    rows = own_ref.shape[1]
    region[...] = jnp.zeros_like(region)
    lane = lax.broadcasted_iota(jnp.int32, (size, size), 1)

    def one_slot(n, carry):
        here = pl.ds(offset_ref[n, 0], size)
        col = offset_ref[n, 1]
        in_first = lane >= col
        for part in range(2):
            term = terms_ref[n, part * size : (part + 1) * size, :]
            turned = pltpu.roll(term, lax.rem(col, size), 1)
            region[part, 0, here, :] = region[part, 0, here, :] + jnp.where(in_first, turned, 0.0)
            region[part, 1, here, :] = region[part, 1, here, :] + jnp.where(in_first, 0.0, turned)
        return carry

    lax.fori_loop(0, slots, one_slot, 0)
    for half in range(2):
        cols = pl.ds(half * size, size)
        own_ref[:, :, cols] = region[:, half, :rows, :]
        band_ref[:, :, cols] = region[:, half, rows:, :]


def add_windows(offsets, terms, rows, width):
    slots, _, size = terms.shape
    vmem = pl.BlockSpec(memory_space=VMEM)
    return pl.pallas_call(
        gather_kernel,
        out_shape=[
            jax.ShapeDtypeStruct((2, rows, width), jnp.float32),
            jax.ShapeDtypeStruct((2, size, width), jnp.float32),
        ],
        in_specs=[pl.BlockSpec(memory_space=SMEM), vmem],
        out_specs=[vmem] * 2,
        scratch_shapes=[VMEM((2, 2, rows + size, size), jnp.float32)],
        compiler_params=pltpu.CompilerParams(vmem_limit_bytes=12 * 2**20),
        name="gather",
    )(offsets, terms)


def passed_along(block, axis, distance):
    count = lax.axis_size(axis)
    return lax.ppermute(block, axis, [((i - distance) % count, i) for i in range(count)])


def per_device(obj_real, obj_imag, probe_real, probe_imag, prop_phase, intensity, offsets, counts):
    size = probe_real.shape[0]
    rows, width = obj_real.shape[1:]
    slot = lax.axis_index("cuts")
    below_real = passed_along(obj_real, "tile", -1)
    below_imag = passed_along(obj_imag, "tile", -1)
    matrices = build_matrices(prop_phase)
    probe = jnp.stack([probe_real, probe_imag])
    measured = lax.dynamic_slice_in_dim(intensity, slot, 1, 0)
    live = (slot < counts).astype(jnp.int32)
    windows = cut_windows(offsets, obj_real, obj_imag, below_real, below_imag, size)
    windows = lax.all_to_all(windows, "cuts", 0, 0, tiled=True)
    terms = run_chain(live, probe, matrices, windows, measured)
    terms = lax.all_to_all(terms, "cuts", 0, 0, tiled=True)
    probe_part = jnp.sum(terms[:, 2 * size :], axis=0)
    tiles = lax.axis_size("tile")
    spread = jnp.broadcast_to(probe_part[None], (tiles,) + probe_part.shape)
    probe_parts = lax.all_to_all(spread, "tile", 0, 0, tiled=True)
    own, band = add_windows(offsets, terms, rows, width)
    band = passed_along(band, "tile", 1)
    probe_grad = jnp.sum(probe_parts, axis=0).reshape(2, -1, size)
    object_grad = (own + band)[:, None]
    return object_grad, probe_grad


def solution(mesh):
    in_specs = (
        P("cuts", "tile", None),
        P("cuts", "tile", None),
        P(),
        P(),
        P(),
        P("tile", None, None),
        P("tile", None),
        P("tile"),
    )
    out_specs = (P(None, "cuts", "tile", None), P(None, "cuts", None))
    return jax.shard_map(
        per_device, mesh=mesh, in_specs=in_specs, out_specs=out_specs, check_vma=False
    )
```

time: 191 us -> 182 us (0.953)
  blocking collectives: 74.1 us -> 56.9 us
  Pallas kernels: 6.84 us -> 20.2 us
  other arithmetic: 9.07 us -> 4.01 us
  starting transfers between devices: 32.8 us -> 35.2 us
    all_to_all x1, blocking collectives: 74.1 us -> 56.9 us  [per_device(): terms = lax.all_to_all(terms, 'cuts', 0, 0, tiled=True)]
    pallas_call x1, Pallas kernels: 0.15 us -> 13.9 us  [run_chain(): pl.pallas_call(chain_kernel, out_shape=jax.ShapeDtypeStruct((slices, rows...]
    ppermute x2 -> x3, waiting for transfers between devices: 18 us -> 13.4 us  [passed_along(): lax.ppermute(block, axis, [((i - distance) % count, i) for i in range(cou...]
    another operation x4 -> x0, other arithmetic: 3.81 us -> none  [the longest x2 2.41 us: build_operators(): jnp.stack([stacked_left(left_operator(s_real, s_imag)), stacked_left(left...]
    all_to_all x1, waiting for transfers between devices: 38.9 us -> 42.7 us  [per_device(): windows = lax.all_to_all(windows, 'cuts', 0, 0, tiled=True)]
    ppermute x2 -> x3, starting transfers between devices: 16.8 us -> 19.4 us  [passed_along(): lax.ppermute(block, axis, [((i - distance) % count, i) for i in range(cou...]
    unnamed x31 -> x26, local copies, waits for them, and re-layouts: 5.62 us -> 4.66 us
  transfers between devices with their start and end apart: 4 -> 5, of which waited for: 3 -> 3; matrix products, arithmetic and copies ran while one was open for 6% -> 4% of each run, Pallas kernels for 0% -> 1%
where the time goes in v2:
time: 182 us; the launch traced here: 181 us
  blocking collectives  56.9 us (31%)
  waiting for transfers between devices  56.1 us (31%)
  starting transfers between devices  35.2 us (19%)
  Pallas kernels  20.2 us (11%)
  local copies, waits for them, and re-layouts  6.25 us (3%)
  other arithmetic  4.01 us (2%)
    all_to_all x1, blocking collectives, per_device(): terms = lax.all_to_all(terms, 'cuts', 0, 0, tiled=True)  56.9 us
    all_to_all x1, waiting for transfers between devices, per_device(): windows = lax.all_to_all(windows, 'cuts', 0, 0, tiled=True)  42.7 us
    ppermute x3, starting transfers between devices, passed_along(): lax.ppermute(block, axis, [((i - distance) % count, i) for i in range(cou...  19.4 us
    pallas_call x1, Pallas kernels, run_chain(): pl.pallas_call(chain_kernel, out_shape=jax.ShapeDtypeStruct((slices, rows...  13.9 us
    ppermute x3, waiting for transfers between devices, passed_along(): lax.ppermute(block, axis, [((i - distance) % count, i) for i in range(cou...  13.4 us
    all_to_all x1, starting transfers between devices, per_device(): windows = lax.all_to_all(windows, 'cuts', 0, 0, tiled=True)  9.36 us
    all_to_all x1, starting transfers between devices, per_device(): probe_parts = lax.all_to_all(spread, 'tile', 0, 0, tiled=True)  6.4 us
    unnamed x26, local copies, waits for them, and re-layouts  4.66 us
  transfers between devices with their start and end apart: 5, of which 3 were waited for; matrix products, arithmetic and copies ran while one was open for 4% of the time, Pallas kernels for 1%

profile of v2, /device:TPU:1, one launch (start us, length us, event | category | flops | bytes accessed | tf_op | source)
XLA Modules:
  0.0 181.3 jit_solution(11478161789124593932)
XLA Ops:
  0.6 0.0 copy-start
  0.6 13.8 %collective-permute-start = (f32[1,128,256]{2,1,0:T(8,128)}, f32[1,128,256]{2,1,0:T(8,128)S(1)}, u32[]{:S(2)}, u32[]{:S(2)}) collective-permute-start(f32[1,128,256]{2,1,0:T(8,128)} %real_hbm.1), channel_id=1, source_target_pairs={{1,0},{2,1},{3,2},{4,3},{5,4},{6,5},{7,6},{8,7},{9,8},{10,9},{11,1... | collective-permute-start | bytes 393224 | tf_op jit(solution)/shard_map/ppermute | solution.py:248
  14.5 2.5 %collective-permute-start.1 = (f32[1,128,256]{2,1,0:T(8,128)}, f32[1,128,256]{2,1,0:T(8,128)S(1)}, u32[]{:S(2)}, u32[]{:S(2)}) collective-permute-start(f32[1,128,256]{2,1,0:T(8,128)} %imag_hbm.1), channel_id=1, source_target_pairs={{1,0},{2,1},{3,2},{4,3},{5,4},{6,5},{7,6},{8,7},{9,8},{10,9},{11,1... | collective-permute-start | bytes 393224 | tf_op jit(solution)/shard_map/ppermute | solution.py:248
  16.9 1.4 copy.31.offset_ref
  18.3 0.0 collective-permute-done.real_below
  18.3 0.0 copy-start.6
  18.3 2.1 %collective-permute-done.1.imag_below = f32[1,128,256]{2,1,0:T(8,128)S(1)} collective-permute-done((f32[1,128,256]{2,1,0:T(8,128)}, f32[1,128,256]{2,1,0:T(8,128)S(1)}, u32[]{:S(2)}, u32[]{:S(2)}) %collective-permute-start.1) | collective-permute-done | bytes 131104 | tf_op jit(solution)/shard_map/ppermute | solution.py:248
  20.4 0.0 copy-done.6
  20.4 0.0 copy-start.7
  20.4 0.6 copy-done.7
  21.1 3.9 %cut.1 = f32[16,256,128]{2,1,0:T(8,128)} custom-call(s32[16,2]{1,0:T(8,128)} %copy.31.offset_ref, f32[1,128,256]{2,1,0:T(8,128)} %real_hbm.1, f32[1,128,256]{2,1,0:T(8,128)} %imag_hbm.1, f32[1,128,256]{2,1,0:T(8,128)} %copy-done.6, f32[1,128,256]{2,1,0:T(8,128)} %copy-done.7), custom_call_target="tpu_custom_call" | custom-call | tf_op jit(solution)/shard_map/cut/pallas_call | solution.py:189
  24.9 0.0 copy-start.9
  24.9 0.0 copy-start.4
  24.9 0.0 copy-start.5
  24.9 0.0 copy-start.8
  25.0 9.4 %all-to-all-start = ((f32[16,256,128]{2,1,0:T(8,128)}), f32[16,256,128]{2,1,0:T(8,128)S(1)}, u32[]{:S(2)}, u32[]{:S(2)}) async-start(f32[16,256,128]{2,1,0:T(8,128)} %cut.1), calls=%async_computation | async-start | bytes 4194304 | tf_op jit(solution)/shard_map/all_to_all | solution.py:262
  35.0 0.0 copy-done.9
  35.0 0.0 copy-done.4
  35.0 0.0 copy-done.5
  35.0 0.3 fusion.2
  35.3 0.3 convolution_add_fusion
  35.6 0.1 copy.29
  35.7 0.3 fusion.3
  36.0 0.3 convolution_subtract_fusion
  36.3 0.1 copy.28
  36.4 0.0 copy-done
  36.5 0.6 constant_dynamic-slice_fusion.refs_2_
  37.1 0.8 constant_dynamic-update-slice_fusion.1
  38.0 0.0 copy-done.8
  38.0 1.5 pad_maximum_fusion.probe_ref
  39.5 1.1 fusion.1
  40.6 42.7 %all-to-all-done.refs_3_ = f32[16,256,128]{2,1,0:T(8,128)S(1)} async-done(((f32[16,256,128]{2,1,0:T(8,128)}), f32[16,256,128]{2,1,0:T(8,128)S(1)}, u32[]{:S(2)}, u32[]{:S(2)}) %all-to-all-start) | async-done | bytes 2097184 | tf_op jit(solution)/shard_map/all_to_all | solution.py:262
  83.3 0.0 copy-start.1
  83.3 0.9 copy-done.1
  84.2 0.0 copy-start.2
  84.2 0.8 copy-done.2
  85.0 13.9 %chain.1 = f32[16,272,128]{2,1,0:T(8,128)S(1)} custom-call(s32[1]{0:T(128)S(6)} %convert_element_type.9.live_ref, f32[2,128,128]{2,1,0:T(8,128)S(1)} %copy-done.1, bf16[6,128,128]{2,1,0:T(8,128)(2,1)S(1)} %get-tuple-element.11.refs_0_, bf16[6,128,128]{2,1,0:T(8,128)(2,1)S(1)} %get-tuple-element.10.refs_1_, f32[1,128,128]{2,1,0:T(8,128)S(1)} %copy-done.2, ...), custom_call_target="tpu_custom_call" | custom-call | tf_op jit(solution)/shard_map/chain/pallas_call | solution.py:131
  98.9 0.0 copy-start.3
  98.9 56.9 %all_to_all.15.terms_ref = f32[16,272,128]{2,1,0:T(8,128)S(1)} all-to-all(f32[16,272,128]{2,1,0:T(8,128)S(1)} %chain.1), channel_id=1, replica_groups=mesh['cuts'=16,'tile'=32] {'cuts'}, dimensions={0} | all-to-all | bytes 4456448 | tf_op jit(solution)/shard_map/all_to_all | solution.py:264
  155.8 0.7 broadcast_in_dim.5
  156.5 6.4 %all-to-all-start.2 = ((f32[32,16,128]{2,1,0:T(8,128)}), f32[32,16,128]{2,1,0:T(8,128)S(1)}, u32[]{:S(2)}, u32[]{:S(2)}) async-start(f32[32,16,128]{2,1,0:T(8,128)} %broadcast_in_dim.5), calls=%async_computation.2 | async-start | bytes 524288 | tf_op jit(solution)/shard_map/all_to_all | solution.py:268
  162.9 0.0 copy-done.3
  163.0 2.5 %gather.1 = (f32[2,128,256]{2,1,0:T(8,128)S(1)}, f32[2,128,256]{2,1,0:T(8,128)S(1)}) custom-call(s32[16,2]{1,0:T(8,128)S(1)} %copy-done.3, f32[16,272,128]{2,1,0:T(8,128)S(1)} %all_to_all.15.terms_ref), custom_call_target="tpu_custom_call" | custom-call | tf_op jit(solution)/shard_map/gather/pallas_call | solution.py:232
  165.4 3.2 %collective-permute-start.2 = (f32[2,128,256]{2,1,0:T(8,128)S(1)}, f32[2,128,256]{2,1,0:T(8,128)S(1)}, u32[]{:S(2)}, u32[]{:S(2)}) collective-permute-start(f32[2,128,256]{2,1,0:T(8,128)S(1)} %get-tuple-element.5), channel_id=1, source_target_pairs={{31,0},{0,1},{1,2},{2,3},{3,4},{4,5},{5,6},{6,7},{7,8},{8,9},{9,10... | collective-permute-start | bytes 786440 | tf_op jit(solution)/shard_map/ppermute | solution.py:248
  168.6 11.3 %collective-permute-done.2 = f32[2,128,256]{2,1,0:T(8,128)S(1)} collective-permute-done((f32[2,128,256]{2,1,0:T(8,128)S(1)}, f32[2,128,256]{2,1,0:T(8,128)S(1)}, u32[]{:S(2)}, u32[]{:S(2)}) %collective-permute-start.2) | collective-permute-done | bytes 262176 | tf_op jit(solution)/shard_map/ppermute | solution.py:248
  179.9 0.7 add_bitcast_fusion
  180.7 0.0 all-to-all-done.2
  180.7 0.6 reduce_sum.19
  (7 shorter events, 0.1 us)
Async XLA Ops:
  0.6 35.8 %copy-start = (f32[16,128,128]{2,1,0:T(8,128)S(1)}, f32[16,128,128]{2,1,0:T(8,128)}, u32[]{:S(2)}) copy-start(f32[16,128,128]{2,1,0:T(8,128)} %param.18) | copy-start | bytes 3145732
  0.6 17.7 %collective-permute-start = (f32[1,128,256]{2,1,0:T(8,128)}, f32[1,128,256]{2,1,0:T(8,128)S(1)}, u32[]{:S(2)}, u32[]{:S(2)}) collective-permute-start(f32[1,128,256]{2,1,0:T(8,128)} %real_hbm.1), channel_id=1, source_target_pairs={{1,0},{2,1},{3,2},{4,3},{5,4},{6,5},{7,6},{8,7},{9,8},{10,9},{11,1... | collective-permute-start | bytes 393224 | tf_op jit(solution)/shard_map/ppermute | solution.py:248
  14.5 5.9 %collective-permute-start.1 = (f32[1,128,256]{2,1,0:T(8,128)}, f32[1,128,256]{2,1,0:T(8,128)S(1)}, u32[]{:S(2)}, u32[]{:S(2)}) collective-permute-start(f32[1,128,256]{2,1,0:T(8,128)} %imag_hbm.1), channel_id=1, source_target_pairs={{1,0},{2,1},{3,2},{4,3},{5,4},{6,5},{7,6},{8,7},{9,8},{10,9},{11,1... | collective-permute-start | bytes 393224 | tf_op jit(solution)/shard_map/ppermute | solution.py:248
  18.3 2.1 %copy-start.6 = (f32[1,128,256]{2,1,0:T(8,128)}, f32[1,128,256]{2,1,0:T(8,128)S(1)}, u32[]{:S(2)}) copy-start(f32[1,128,256]{2,1,0:T(8,128)S(1)} %collective-permute-done.real_below) | copy-start | bytes 393220
  20.4 0.6 copy-start.7
  24.9 10.1 %copy-start.9 = (f32[128]{0:T(128)S(1)}, f32[128]{0:T(128)}, u32[]{:S(2)}) copy-start(f32[128]{0:T(128)} %param.17) | copy-start | bytes 1540
  24.9 10.1 %copy-start.4 = (f32[128,128]{1,0:T(8,128)S(1)}, f32[128,128]{1,0:T(8,128)}, u32[]{:S(2)}) copy-start(f32[128,128]{1,0:T(8,128)} %constant.19.clone) | copy-start | bytes 196612
  24.9 10.1 %copy-start.5 = (f32[128,128]{1,0:T(8,128)S(1)}, f32[128,128]{1,0:T(8,128)}, u32[]{:S(2)}) copy-start(f32[128,128]{1,0:T(8,128)} %constant.18.clone) | copy-start | bytes 196612
  24.9 13.0 %copy-start.8 = (f32[1,128,128]{2,1,0:T(8,128)S(1)}, f32[1,128,128]{2,1,0:T(8,128)}, u32[]{:S(2)}) copy-start(f32[1,128,128]{2,1,0:T(8,128)} %constant.27) | copy-start | bytes 196612
  25.0 58.3 %all-to-all-start = ((f32[16,256,128]{2,1,0:T(8,128)}), f32[16,256,128]{2,1,0:T(8,128)S(1)}, u32[]{:S(2)}, u32[]{:S(2)}) async-start(f32[16,256,128]{2,1,0:T(8,128)} %cut.1), calls=%async_computation | async-start | bytes 4194304 | tf_op jit(solution)/shard_map/all_to_all | solution.py:262
  83.3 0.9 copy-start.1
  84.2 0.8 copy-start.2
  98.9 64.0 %copy-start.3 = (s32[16,2]{1,0:T(8,128)S(1)}, s32[16,2]{1,0:T(8,128)}, u32[]{:S(2)}) copy-start(s32[16,2]{1,0:T(8,128)} %copy.31.offset_ref) | copy-start | bytes 388
  156.5 24.1 %all-to-all-start.2 = ((f32[32,16,128]{2,1,0:T(8,128)}), f32[32,16,128]{2,1,0:T(8,128)S(1)}, u32[]{:S(2)}, u32[]{:S(2)}) async-start(f32[32,16,128]{2,1,0:T(8,128)} %broadcast_in_dim.5), calls=%async_computation.2 | async-start | bytes 524288 | tf_op jit(solution)/shard_map/all_to_all | solution.py:268
  165.4 14.5 %collective-permute-start.2 = (f32[2,128,256]{2,1,0:T(8,128)S(1)}, f32[2,128,256]{2,1,0:T(8,128)S(1)}, u32[]{:S(2)}, u32[]{:S(2)}) collective-permute-start(f32[2,128,256]{2,1,0:T(8,128)S(1)} %get-tuple-element.5), channel_id=1, source_target_pairs={{31,0},{0,1},{1,2},{2,3},{3,4},{4,5},{5,6},{6,7},{7,8},{8,9},{9,10... | collective-permute-start | bytes 786440 | tf_op jit(solution)/shard_map/ppermute | solution.py:248

commit v3 on v2

--- a/solution.py
+++ b/solution.py
@@ -30,36 +30,44 @@
     return (np.cos(angle) * scale).astype(np.float32), (-np.sin(angle) * scale).astype(np.float32)
 
 
-def rounded_split(matrix, seed):
-    high = lax.reduce_precision(matrix, 8, 7)
-    dither = np.random.default_rng(seed).uniform(-1.0, 1.0, matrix.shape) * 0.003
-    low = (matrix - high) * (1.0 + dither).astype(np.float32)
-    return high.astype(jnp.bfloat16), low.astype(jnp.bfloat16)
-
-
-def build_matrices(prop_phase):
-    size = prop_phase.shape[0]
-    f_real, f_imag = fourier_pair(size)
-    k_real = jnp.cos(prop_phase)[None, :]
-    k_imag = jnp.sin(prop_phase)[None, :]
+def matrix_kernel(phase_ref, fourier_ref, dither_ref, matrix_ref):
+    f_real, f_imag = fourier_ref[0], fourier_ref[1]
+    phase = phase_ref[...]
+    k_real, k_imag = jnp.cos(phase), jnp.sin(phase)
     l_real = f_real * k_real + f_imag * k_imag
     l_imag = f_real * k_imag - f_imag * k_real
     s_real = exact_dot(l_real, f_real) - exact_dot(l_imag, f_imag)
     s_imag = exact_dot(l_real, f_imag) + exact_dot(l_imag, f_real)
-    return rounded_split(jnp.stack([s_real, s_imag, s_real.T, s_imag.T, f_real, f_imag]), 1)
-
-
-def assemble(matrix_ref, right_ref, left_ref):
+    for k, matrix in enumerate((s_real, s_imag, s_real.T, s_imag.T, f_real, f_imag)):
+        high = matrix.astype(jnp.bfloat16)
+        low = (matrix - high.astype(jnp.float32)) * (1.0 + dither_ref[k % 2])
+        matrix_ref[k] = high
+        matrix_ref[k + 6] = low.astype(jnp.bfloat16)
+
+
+def build_matrices(prop_phase):
+    size = prop_phase.shape[0]
+    dither = np.random.default_rng(1).uniform(-0.003, 0.003, (2, size, size)).astype(np.float32)
+    return pl.pallas_call(
+        matrix_kernel,
+        out_shape=jax.ShapeDtypeStruct((12, size, size), jnp.bfloat16),
+        in_specs=[pl.BlockSpec(memory_space=VMEM)] * 3,
+        out_specs=pl.BlockSpec(memory_space=VMEM),
+        name="matrices",
+    )(prop_phase[None], np.stack(fourier_pair(size)), dither)
+
+
+def assemble(matrix_ref, first, right_ref, left_ref):
     size = matrix_ref.shape[1]
     uses = ((0, 2, 1.0), (4, 4, 1.0), (4, 4, -1.0), (2, 0, -1.0))
     for which, (left, right, sign) in enumerate(uses):
-        real, imag = matrix_ref[right], matrix_ref[right + 1] * sign
+        real, imag = matrix_ref[first + right], matrix_ref[first + right + 1] * sign
         right_ref[which, :size, :size] = real
         right_ref[which, :size, size:] = imag
         right_ref[which, size:, :size] = -imag
         right_ref[which, size:, size:] = real
-        left_ref[which, :, :size] = matrix_ref[left]
-        left_ref[which, :, size:] = matrix_ref[left + 1] * sign
+        left_ref[which, :, :size] = matrix_ref[first + left]
+        left_ref[which, :, size:] = matrix_ref[first + left + 1] * sign
 
 
 def sandwich(wide, operators, which):
@@ -68,16 +76,20 @@
     size = wide.shape[0]
     high, low = split_bf16(wide)
     middle = dot(high, right_high) + dot(low, right_high) + dot(high, right_low)
-    swapped = jnp.concatenate([-middle[:, size:], middle[:, :size]], axis=1)
-    high, low = split_bf16(jnp.concatenate([middle, swapped], axis=0))
+    high, low = (
+        jnp.concatenate(
+            [half, jnp.concatenate([-half[:, size:], half[:, :size]], axis=1)], axis=0
+        )
+        for half in split_bf16(middle)
+    )
     out = dot(left_high, high) + dot(left_low, high) + dot(left_high, low)
     return out[:, :size], out[:, size:]
 
 
-def chain_kernel(live_ref, probe_ref, *refs):
-    high_ref, low_ref, measured_ref, window_ref, out_ref, waves, *operators = refs
+def chain_kernel(live_ref, probe_real, probe_imag, *refs):
+    matrix_ref, measured_ref, window_ref, out_ref, waves, *operators = refs
     slices = window_ref.shape[0]
-    size = probe_ref.shape[1]
+    size = probe_real.shape[0]
     extra = size // slices
     live = live_ref[0] > 0
 
@@ -87,8 +99,8 @@
 
     @pl.when(live)
     def _():
-        assemble(high_ref, operators[0], operators[2])
-        assemble(low_ref, operators[1], operators[3])
+        assemble(matrix_ref, 0, operators[0], operators[2])
+        assemble(matrix_ref, 6, operators[1], operators[3])
 
         def modulated(s, real, imag):
             waves[s, :size, :] = real
@@ -99,7 +111,7 @@
                 [real * p_real - imag * p_imag, real * p_imag + imag * p_real], axis=1
             )
 
-        state = (probe_ref[0], probe_ref[1])
+        state = (probe_real[...], probe_imag[...])
         for s in range(slices - 1):
             state = sandwich(modulated(s, *state), operators, 0)
         wide = modulated(slices - 1, *state)
@@ -124,7 +136,7 @@
             out_ref[s, 2 * size + extra :, :] = g_i[s * extra : (s + 1) * extra]
 
 
-def run_chain(live, probe, matrices, windows, measured):
+def run_chain(live, probe_real, probe_imag, matrices, windows, measured):
     slices, _, size = windows.shape
     rows = 2 * size + 2 * (size // slices)
     vmem = pl.BlockSpec(memory_space=VMEM)
@@ -142,11 +154,11 @@
         ],
         compiler_params=pltpu.CompilerParams(vmem_limit_bytes=16 * 2**20),
         name="chain",
-    )(live, probe, *matrices, measured, windows)
+    )(live, probe_real, probe_imag, matrices, measured, windows)
 
 
 def cut_kernel(
-    offset_ref, real_hbm, imag_hbm, real_below, imag_below, out_hbm, region, out_ref, sems, out_sems
+    offset_ref, real_hbm, imag_hbm, real_below, imag_below, out_ref, region, sems
 ):
     slots, _, size = out_ref.shape
     rows = real_hbm.shape[1]
@@ -175,12 +187,9 @@
         for part in range(2):
             mixed = jnp.where(in_first, region[part, 0, here, :], region[part, 1, here, :])
             out_ref[n, part * size : (part + 1) * size, :] = pltpu.roll(mixed, shift, 1)
-        pltpu.make_async_copy(out_ref.at[n], out_hbm.at[n], out_sems.at[n]).start()
         return carry
 
     lax.fori_loop(0, slots, one_slot, 0, unroll=2)
-    for n in range(slots):
-        pltpu.make_async_copy(out_ref.at[n], out_hbm.at[n], out_sems.at[n]).wait()
 
 
 def cut_windows(offsets, obj_real, obj_imag, below_real, below_imag, size):
@@ -190,14 +199,12 @@
         cut_kernel,
         out_shape=jax.ShapeDtypeStruct((slots, 2 * size, size), jnp.float32),
         in_specs=[pl.BlockSpec(memory_space=SMEM)] + [pl.BlockSpec(memory_space=pl.ANY)] * 4,
-        out_specs=pl.BlockSpec(memory_space=pl.ANY),
+        out_specs=pl.BlockSpec(memory_space=VMEM),
         scratch_shapes=[
             VMEM((2, 2, 2 * rows, size), jnp.float32),
-            VMEM((slots, 2 * size, size), jnp.float32),
             pltpu.SemaphoreType.DMA((8,)),
-            pltpu.SemaphoreType.DMA((slots,)),
         ],
-        compiler_params=pltpu.CompilerParams(vmem_limit_bytes=60 * 2**20),
+        compiler_params=pltpu.CompilerParams(vmem_limit_bytes=12 * 2**20),
         name="cut",
     )(offsets, obj_real, obj_imag, below_real, below_imag)
 
@@ -219,7 +226,7 @@
             region[part, 1, here, :] = region[part, 1, here, :] + jnp.where(in_first, 0.0, turned)
         return carry
 
-    lax.fori_loop(0, slots, one_slot, 0)
+    lax.fori_loop(0, slots, one_slot, 0, unroll=2)
     for half in range(2):
         cols = pl.ds(half * size, size)
         own_ref[:, :, cols] = region[:, half, :rows, :]
@@ -255,12 +262,14 @@
     below_real = passed_along(obj_real, "tile", -1)
     below_imag = passed_along(obj_imag, "tile", -1)
     matrices = build_matrices(prop_phase)
-    probe = jnp.stack([probe_real, probe_imag])
     measured = lax.dynamic_slice_in_dim(intensity, slot, 1, 0)
     live = (slot < counts).astype(jnp.int32)
+    below_real, below_imag, matrices, measured, live = lax.optimization_barrier(
+        (below_real, below_imag, matrices, measured, live)
+    )
     windows = cut_windows(offsets, obj_real, obj_imag, below_real, below_imag, size)
     windows = lax.all_to_all(windows, "cuts", 0, 0, tiled=True)
-    terms = run_chain(live, probe, matrices, windows, measured)
+    terms = run_chain(live, probe_real, probe_imag, matrices, windows, measured)
     terms = lax.all_to_all(terms, "cuts", 0, 0, tiled=True)
     probe_part = jnp.sum(terms[:, 2 * size :], axis=0)
     tiles = lax.axis_size("tile")

time: 182 us -> 180 us (0.989)
  blocking collectives: 56.9 us -> 116 us
  waiting for transfers between devices: 56.1 us -> 12.1 us
  starting transfers between devices: 35.2 us -> 26.2 us
  local copies, waits for them, and re-layouts: 6.25 us -> 3.31 us
  other arithmetic: 4.01 us -> 1.39 us
    all_to_all x0 -> x1, blocking collectives: none -> 59.9 us  [per_device(): windows = lax.all_to_all(windows, 'cuts', 0, 0, tiled=True)]
    all_to_all x1 -> x0, waiting for transfers between devices: 42.7 us -> none  [per_device(): windows = lax.all_to_all(windows, 'cuts', 0, 0, tiled=True)]
    all_to_all x1 -> x0, starting transfers between devices: 9.36 us -> none  [per_device(): windows = lax.all_to_all(windows, 'cuts', 0, 0, tiled=True)]
    pallas_call x0 -> x1, Pallas kernels: none -> 2.24 us  [build_matrices(): pl.pallas_call(matrix_kernel, out_shape=jax.ShapeDtypeStruct((12, size, s...]
    unnamed x26 -> x13, local copies, waits for them, and re-layouts: 4.66 us -> 2.59 us
    pallas_call x1, Pallas kernels: 3.85 us -> 1.9 us  [cut_windows(): pl.pallas_call(cut_kernel, out_shape=jax.ShapeDtypeStruct((slots, 2 * siz...]
  transfers between devices with their start and end apart: 5 -> 4, of which waited for: 3 -> 1; matrix products, arithmetic and copies ran while one was open for 4% -> 1% of each run, Pallas kernels for 1% -> 2%
where the time goes in v3:
time: 180 us
  blocking collectives  116 us (64%)
  starting transfers between devices  26.2 us (15%)
  Pallas kernels  19.9 us (11%)
  waiting for transfers between devices  12.1 us (7%)
  local copies, waits for them, and re-layouts  3.31 us (2%)
    all_to_all x1, blocking collectives, per_device(): windows = lax.all_to_all(windows, 'cuts', 0, 0, tiled=True)  59.9 us
    all_to_all x1, blocking collectives, per_device(): terms = lax.all_to_all(terms, 'cuts', 0, 0, tiled=True)  55.6 us
    ppermute x3, starting transfers between devices, passed_along(): lax.ppermute(block, axis, [((i - distance) % count, i) for i in range(cou...  19.4 us
    pallas_call x1, Pallas kernels, run_chain(): pl.pallas_call(chain_kernel, out_shape=jax.ShapeDtypeStruct((slices, rows...  13.9 us
    ppermute x3, waiting for transfers between devices, passed_along(): lax.ppermute(block, axis, [((i - distance) % count, i) for i in range(cou...  12.1 us
    all_to_all x1, starting transfers between devices, per_device(): probe_parts = lax.all_to_all(spread, 'tile', 0, 0, tiled=True)  6.8 us
  transfers between devices with their start and end apart: 4, of which 1 were waited for; matrix products, arithmetic and copies ran while one was open for 1% of the time, Pallas kernels for 2%

profile of v3, /device:TPU:1, one launch (start us, length us, event | category | flops | bytes accessed | tf_op | source)
XLA Modules:
  0.0 179.9 jit_solution(940337721101647702)
XLA Ops:
  0.6 0.0 copy-start
  0.6 13.8 %collective-permute-start = (f32[1,128,256]{2,1,0:T(8,128)}, f32[1,128,256]{2,1,0:T(8,128)S(1)}, u32[]{:S(2)}, u32[]{:S(2)}) collective-permute-start(f32[1,128,256]{2,1,0:T(8,128)} %real_hbm.1), channel_id=1, source_target_pairs={{1,0},{2,1},{3,2},{4,3},{5,4},{6,5},{7,6},{8,7},{9,8},{10,9},{11,1... | collective-permute-start | bytes 393224 | tf_op jit(solution)/shard_map/ppermute | solution.py:255
  14.5 2.5 %collective-permute-start.1 = (f32[1,128,256]{2,1,0:T(8,128)}, f32[1,128,256]{2,1,0:T(8,128)S(1)}, u32[]{:S(2)}, u32[]{:S(2)}) collective-permute-start(f32[1,128,256]{2,1,0:T(8,128)} %imag_hbm.1), channel_id=1, source_target_pairs={{1,0},{2,1},{3,2},{4,3},{5,4},{6,5},{7,6},{8,7},{9,8},{10,9},{11,1... | collective-permute-start | bytes 393224 | tf_op jit(solution)/shard_map/ppermute | solution.py:255
  17.6 0.8 copy.16.offset_ref
  18.4 2.2 %matrices.1.refs_0_ = bf16[12,128,128]{2,1,0:T(8,128)(2,1)} custom-call(f32[1,128]{1,0:T(1,128)} %bitcast.8, f32[2,128,128]{2,1,0:T(8,128)} %constant.16.clone.fourier_ref, f32[2,128,128]{2,1,0:T(8,128)} %constant.17.clone.dither_ref), custom_call_target="tpu_custom_call" | custom-call | tf_op jit(solution)/shard_map/matrices/pallas_call | solution.py:51
  20.6 0.0 copy-done
  20.6 0.0 collective-permute-done.real_below
  20.6 0.0 collective-permute-done.1.imag_below
  20.6 0.0 copy-start.2
  20.6 0.9 copy-done.2
  21.5 0.0 copy-start.3
  21.5 0.9 copy-done.3
  22.4 1.9 %cut.1 = f32[16,256,128]{2,1,0:T(8,128)S(1)} custom-call(s32[16,2]{1,0:T(8,128)S(1)} %copy.16.offset_ref, f32[1,128,256]{2,1,0:T(8,128)S(1)} %copy-done.2, f32[1,128,256]{2,1,0:T(8,128)S(1)} %copy-done.3, f32[1,128,256]{2,1,0:T(8,128)S(1)} %collective-permute-done.real_below, f32[1,128,256]{2,1,0:T(8,128)S(1)} %collective-permute-done.1.imag_below), custom_call_target="tpu_custom_call" | custom-call | tf_op jit(solution)/shard_map/cut/pallas_call | solution.py:198
  24.3 0.0 copy-start.1
  24.4 0.0 copy-start.4
  24.4 0.0 copy-start.5
  24.4 59.9 %all_to_all.15.refs_2_ = f32[16,256,128]{2,1,0:T(8,128)S(1)} all-to-all(f32[16,256,128]{2,1,0:T(8,128)S(1)} %cut.1), channel_id=1, replica_groups=mesh['cuts'=16,'tile'=32] {'cuts'}, dimensions={0} | all-to-all | bytes 4194304 | tf_op jit(solution)/shard_map/all_to_all | solution.py:271
  84.3 0.0 copy-done.1
  84.3 0.0 copy-done.4
  84.3 0.0 copy-done.5
  84.3 13.9 %chain.1 = f32[16,272,128]{2,1,0:T(8,128)S(1)} custom-call(s32[1]{0:T(128)S(6)} %convert_element_type.3.live_ref, f32[128,128]{1,0:T(8,128)S(1)} %copy-done.4, f32[128,128]{1,0:T(8,128)S(1)} %copy-done.5, bf16[12,128,128]{2,1,0:T(8,128)(2,1)S(1)} %copy-done.1, f32[1,128,128]{2,1,0:T(8,128)S(1)} %constant_dynamic-slice_fusion.refs_1_, ...), custom_call_target="tpu_custom_call" | custom-call | tf_op jit(solution)/shard_map/chain/pallas_call | solution.py:143
  98.2 55.6 %all_to_all.16.terms_ref = f32[16,272,128]{2,1,0:T(8,128)S(1)} all-to-all(f32[16,272,128]{2,1,0:T(8,128)S(1)} %chain.1), channel_id=1, replica_groups=mesh['cuts'=16,'tile'=32] {'cuts'}, dimensions={0} | all-to-all | bytes 4456448 | tf_op jit(solution)/shard_map/all_to_all | solution.py:273
  153.8 0.7 broadcast_in_dim.14
  154.6 6.8 %all-to-all-start.2 = ((f32[32,16,128]{2,1,0:T(8,128)}), f32[32,16,128]{2,1,0:T(8,128)S(1)}, u32[]{:S(2)}, u32[]{:S(2)}) async-start(f32[32,16,128]{2,1,0:T(8,128)} %broadcast_in_dim.14), calls=%async_computation.2 | async-start | bytes 524288 | tf_op jit(solution)/shard_map/all_to_all | solution.py:277
  161.4 1.9 %gather.1 = (f32[2,128,256]{2,1,0:T(8,128)S(1)}, f32[2,128,256]{2,1,0:T(8,128)S(1)}) custom-call(s32[16,2]{1,0:T(8,128)S(1)} %copy.16.offset_ref, f32[16,272,128]{2,1,0:T(8,128)S(1)} %all_to_all.16.terms_ref), custom_call_target="tpu_custom_call" | custom-call | tf_op jit(solution)/shard_map/gather/pallas_call | solution.py:239
  163.3 3.2 %collective-permute-start.2 = (f32[2,128,256]{2,1,0:T(8,128)S(1)}, f32[2,128,256]{2,1,0:T(8,128)S(1)}, u32[]{:S(2)}, u32[]{:S(2)}) collective-permute-start(f32[2,128,256]{2,1,0:T(8,128)S(1)} %get-tuple-element.15), channel_id=1, source_target_pairs={{31,0},{0,1},{1,2},{2,3},{3,4},{4,5},{5,6},{6,7},{7,8},{8,9},{9,10... | collective-permute-start | bytes 786440 | tf_op jit(solution)/shard_map/ppermute | solution.py:255
  166.4 12.1 %collective-permute-done.2 = f32[2,128,256]{2,1,0:T(8,128)S(1)} collective-permute-done((f32[2,128,256]{2,1,0:T(8,128)S(1)}, f32[2,128,256]{2,1,0:T(8,128)S(1)}, u32[]{:S(2)}, u32[]{:S(2)}) %collective-permute-start.2) | collective-permute-done | bytes 262176 | tf_op jit(solution)/shard_map/ppermute | solution.py:255
  178.5 0.7 add_bitcast_fusion
  179.2 0.0 all-to-all-done.2
  179.2 0.6 reduce_sum.19
  (2 shorter events, 0.0 us)
Async XLA Ops:
  0.6 20.0 %copy-start = (f32[16,128,128]{2,1,0:T(8,128)S(1)}, f32[16,128,128]{2,1,0:T(8,128)}, u32[]{:S(2)}) copy-start(f32[16,128,128]{2,1,0:T(8,128)} %param.15) | copy-start | bytes 3145732
  0.6 20.0 %collective-permute-start = (f32[1,128,256]{2,1,0:T(8,128)}, f32[1,128,256]{2,1,0:T(8,128)S(1)}, u32[]{:S(2)}, u32[]{:S(2)}) collective-permute-start(f32[1,128,256]{2,1,0:T(8,128)} %real_hbm.1), channel_id=1, source_target_pairs={{1,0},{2,1},{3,2},{4,3},{5,4},{6,5},{7,6},{8,7},{9,8},{10,9},{11,1... | collective-permute-start | bytes 393224 | tf_op jit(solution)/shard_map/ppermute | solution.py:255
  14.5 6.1 %collective-permute-start.1 = (f32[1,128,256]{2,1,0:T(8,128)}, f32[1,128,256]{2,1,0:T(8,128)S(1)}, u32[]{:S(2)}, u32[]{:S(2)}) collective-permute-start(f32[1,128,256]{2,1,0:T(8,128)} %imag_hbm.1), channel_id=1, source_target_pairs={{1,0},{2,1},{3,2},{4,3},{5,4},{6,5},{7,6},{8,7},{9,8},{10,9},{11,1... | collective-permute-start | bytes 393224 | tf_op jit(solution)/shard_map/ppermute | solution.py:255
  20.6 0.9 copy-start.2
  21.5 0.9 copy-start.3
  24.3 60.0 %copy-start.1 = (bf16[12,128,128]{2,1,0:T(8,128)(2,1)S(1)}, bf16[12,128,128]{2,1,0:T(8,128)(2,1)}, u32[]{:S(2)}) copy-start(bf16[12,128,128]{2,1,0:T(8,128)(2,1)} %matrices.1.refs_0_) | copy-start | bytes 1179652
  24.4 60.0 %copy-start.4 = (f32[128,128]{1,0:T(8,128)S(1)}, f32[128,128]{1,0:T(8,128)}, u32[]{:S(2)}) copy-start(f32[128,128]{1,0:T(8,128)} %probe_real.1) | copy-start | bytes 196612
  24.4 60.0 %copy-start.5 = (f32[128,128]{1,0:T(8,128)S(1)}, f32[128,128]{1,0:T(8,128)}, u32[]{:S(2)}) copy-start(f32[128,128]{1,0:T(8,128)} %probe_imag.1) | copy-start | bytes 196612
  154.6 24.7 %all-to-all-start.2 = ((f32[32,16,128]{2,1,0:T(8,128)}), f32[32,16,128]{2,1,0:T(8,128)S(1)}, u32[]{:S(2)}, u32[]{:S(2)}) async-start(f32[32,16,128]{2,1,0:T(8,128)} %broadcast_in_dim.14), calls=%async_computation.2 | async-start | bytes 524288 | tf_op jit(solution)/shard_map/all_to_all | solution.py:277
  163.3 15.2 %collective-permute-start.2 = (f32[2,128,256]{2,1,0:T(8,128)S(1)}, f32[2,128,256]{2,1,0:T(8,128)S(1)}, u32[]{:S(2)}, u32[]{:S(2)}) collective-permute-start(f32[2,128,256]{2,1,0:T(8,128)S(1)} %get-tuple-element.15), channel_id=1, source_target_pairs={{31,0},{0,1},{1,2},{2,3},{3,4},{4,5},{5,6},{6,7},{7,8},{8,9},{9,10... | collective-permute-start | bytes 786440 | tf_op jit(solution)/shard_map/ppermute | solution.py:255

commit v4 on v3

--- a/solution.py
+++ b/solution.py
@@ -30,7 +30,12 @@
     return (np.cos(angle) * scale).astype(np.float32), (-np.sin(angle) * scale).astype(np.float32)
 
 
-def matrix_kernel(phase_ref, fourier_ref, dither_ref, matrix_ref):
+def prepare_kernel(phase_ref, fourier_ref, dither_ref, real_ref, imag_ref, matrix_ref, own_ref):
+    size = matrix_ref.shape[1]
+    for half in range(2):
+        cols = pl.ds(half * size, size)
+        own_ref[0, half] = real_ref[0, :, cols]
+        own_ref[1, half] = imag_ref[0, :, cols]
     f_real, f_imag = fourier_ref[0], fourier_ref[1]
     phase = phase_ref[...]
     k_real, k_imag = jnp.cos(phase), jnp.sin(phase)
@@ -45,16 +50,20 @@
         matrix_ref[k + 6] = low.astype(jnp.bfloat16)
 
 
-def build_matrices(prop_phase):
+def prepare(prop_phase, obj_real, obj_imag):
     size = prop_phase.shape[0]
+    rows = obj_real.shape[1]
     dither = np.random.default_rng(1).uniform(-0.003, 0.003, (2, size, size)).astype(np.float32)
     return pl.pallas_call(
-        matrix_kernel,
-        out_shape=jax.ShapeDtypeStruct((12, size, size), jnp.bfloat16),
-        in_specs=[pl.BlockSpec(memory_space=VMEM)] * 3,
-        out_specs=pl.BlockSpec(memory_space=VMEM),
-        name="matrices",
-    )(prop_phase[None], np.stack(fourier_pair(size)), dither)
+        prepare_kernel,
+        out_shape=[
+            jax.ShapeDtypeStruct((12, size, size), jnp.bfloat16),
+            jax.ShapeDtypeStruct((2, 2, rows, size), jnp.float32),
+        ],
+        in_specs=[pl.BlockSpec(memory_space=VMEM)] * 5,
+        out_specs=[pl.BlockSpec(memory_space=VMEM)] * 2,
+        name="prepare",
+    )(prop_phase[None], np.stack(fourier_pair(size)), dither, obj_real, obj_imag)
 
 
 def assemble(matrix_ref, first, right_ref, left_ref):
@@ -75,7 +84,10 @@
     right_high, right_low, left_high, left_low = (ref[which] for ref in operators)
     size = wide.shape[0]
     high, low = split_bf16(wide)
-    middle = dot(high, right_high) + dot(low, right_high) + dot(high, right_low)
+    middle = dot(
+        jnp.concatenate([high, low, high], axis=1),
+        jnp.concatenate([right_high, right_high, right_low], axis=0),
+    )
     high, low = (
         jnp.concatenate(
             [half, jnp.concatenate([-half[:, size:], half[:, :size]], axis=1)], axis=0
@@ -157,26 +169,14 @@
     )(live, probe_real, probe_imag, matrices, measured, windows)
 
 
-def cut_kernel(
-    offset_ref, real_hbm, imag_hbm, real_below, imag_below, out_ref, region, sems
-):
+def cut_kernel(offset_ref, own_ref, real_below, imag_below, out_ref, region):
     slots, _, size = out_ref.shape
-    rows = real_hbm.shape[1]
-    parts = ((0, 0, real_hbm), (1, 0, imag_hbm), (0, rows, real_below), (1, rows, imag_below))
-    arrivals = []
-    for part, first, source in parts:
-        for half in range(2):
-            arrivals.append(
-                pltpu.make_async_copy(
-                    source.at[0, :, pl.ds(half * size, size)],
-                    region.at[part, half, pl.ds(first, rows)],
-                    sems.at[len(arrivals)],
-                )
-            )
-    for arrival in arrivals:
-        arrival.start()
-    for arrival in arrivals:
-        arrival.wait()
+    rows = own_ref.shape[2]
+    region[:, :, :rows, :] = own_ref[...]
+    for half in range(2):
+        cols = pl.ds(half * size, size)
+        region[0, half, rows:, :] = real_below[0, :, cols]
+        region[1, half, rows:, :] = imag_below[0, :, cols]
     lane = lax.broadcasted_iota(jnp.int32, (size, size), 1)
 
     def one_slot(n, carry):
@@ -192,21 +192,19 @@
     lax.fori_loop(0, slots, one_slot, 0, unroll=2)
 
 
-def cut_windows(offsets, obj_real, obj_imag, below_real, below_imag, size):
+def cut_windows(offsets, own, below_real, below_imag):
     slots = offsets.shape[0]
-    _, rows, width = obj_real.shape
+    _, _, rows, size = own.shape
+    vmem = pl.BlockSpec(memory_space=VMEM)
     return pl.pallas_call(
         cut_kernel,
         out_shape=jax.ShapeDtypeStruct((slots, 2 * size, size), jnp.float32),
-        in_specs=[pl.BlockSpec(memory_space=SMEM)] + [pl.BlockSpec(memory_space=pl.ANY)] * 4,
-        out_specs=pl.BlockSpec(memory_space=VMEM),
-        scratch_shapes=[
-            VMEM((2, 2, 2 * rows, size), jnp.float32),
-            pltpu.SemaphoreType.DMA((8,)),
-        ],
+        in_specs=[pl.BlockSpec(memory_space=SMEM)] + [vmem] * 3,
+        out_specs=vmem,
+        scratch_shapes=[VMEM((2, 2, 2 * rows, size), jnp.float32)],
         compiler_params=pltpu.CompilerParams(vmem_limit_bytes=12 * 2**20),
         name="cut",
-    )(offsets, obj_real, obj_imag, below_real, below_imag)
+    )(offsets, own, below_real, below_imag)
 
 
 def gather_kernel(offset_ref, terms_ref, own_ref, band_ref, region):
@@ -261,13 +259,13 @@
     slot = lax.axis_index("cuts")
     below_real = passed_along(obj_real, "tile", -1)
     below_imag = passed_along(obj_imag, "tile", -1)
-    matrices = build_matrices(prop_phase)
+    matrices, own_rows = prepare(prop_phase, obj_real, obj_imag)
     measured = lax.dynamic_slice_in_dim(intensity, slot, 1, 0)
     live = (slot < counts).astype(jnp.int32)
-    below_real, below_imag, matrices, measured, live = lax.optimization_barrier(
-        (below_real, below_imag, matrices, measured, live)
-    )
-    windows = cut_windows(offsets, obj_real, obj_imag, below_real, below_imag, size)
+    below_real, below_imag, matrices, own_rows, measured, live = lax.optimization_barrier(
+        (below_real, below_imag, matrices, own_rows, measured, live)
+    )
+    windows = cut_windows(offsets, own_rows, below_real, below_imag)
     windows = lax.all_to_all(windows, "cuts", 0, 0, tiled=True)
     terms = run_chain(live, probe_real, probe_imag, matrices, windows, measured)
     terms = lax.all_to_all(terms, "cuts", 0, 0, tiled=True)

time: 180 us -> 178 us (0.989)
  no operation moved by 1% of the time
where the time goes in v4:
time: 178 us
  blocking collectives  115 us (65%)
  starting transfers between devices  25.4 us (14%)
  Pallas kernels  19.8 us (11%)
  waiting for transfers between devices  12 us (7%)
  local copies, waits for them, and re-layouts  2.45 us (1%)
    all_to_all x1, blocking collectives, per_device(): windows = lax.all_to_all(windows, 'cuts', 0, 0, tiled=True)  59.8 us
    all_to_all x1, blocking collectives, per_device(): terms = lax.all_to_all(terms, 'cuts', 0, 0, tiled=True)  55.5 us
    ppermute x3, starting transfers between devices, passed_along(): lax.ppermute(block, axis, [((i - distance) % count, i) for i in range(cou...  19.4 us
    pallas_call x1, Pallas kernels, run_chain(): pl.pallas_call(chain_kernel, out_shape=jax.ShapeDtypeStruct((slices, rows...  13.8 us
    ppermute x3, waiting for transfers between devices, passed_along(): lax.ppermute(block, axis, [((i - distance) % count, i) for i in range(cou...  12 us
    all_to_all x1, starting transfers between devices, per_device(): probe_parts = lax.all_to_all(spread, 'tile', 0, 0, tiled=True)  5.93 us
  transfers between devices with their start and end apart: 4, of which 1 were waited for; matrix products, arithmetic and copies ran while one was open for 1% of the time, Pallas kernels for 2%

profile of v4, /device:TPU:1, one launch (start us, length us, event | category | flops | bytes accessed | tf_op | source)
XLA Modules:
  0.0 177.7 jit_solution(6230800071821060056)
XLA Ops:
  0.6 0.0 copy-start
  0.6 13.8 %collective-permute-start = (f32[1,128,256]{2,1,0:T(8,128)}, f32[1,128,256]{2,1,0:T(8,128)S(1)}, u32[]{:S(2)}, u32[]{:S(2)}) collective-permute-start(f32[1,128,256]{2,1,0:T(8,128)} %real_ref.1), channel_id=1, source_target_pairs={{1,0},{2,1},{3,2},{4,3},{5,4},{6,5},{7,6},{8,7},{9,8},{10,9},{11,1... | collective-permute-start | bytes 393224 | tf_op jit(solution)/shard_map/ppermute | solution.py:253
  14.5 2.5 %collective-permute-start.1 = (f32[1,128,256]{2,1,0:T(8,128)}, f32[1,128,256]{2,1,0:T(8,128)S(1)}, u32[]{:S(2)}, u32[]{:S(2)}) collective-permute-start(f32[1,128,256]{2,1,0:T(8,128)} %imag_ref.1), channel_id=1, source_target_pairs={{1,0},{2,1},{3,2},{4,3},{5,4},{6,5},{7,6},{8,7},{9,8},{10,9},{11,1... | collective-permute-start | bytes 393224 | tf_op jit(solution)/shard_map/ppermute | solution.py:253
  17.6 0.8 copy.16.offset_ref
  18.4 2.4 %prepare.1 = (bf16[12,128,128]{2,1,0:T(8,128)(2,1)}, f32[2,2,128,128]{3,2,1,0:T(8,128)}) custom-call(f32[1,128]{1,0:T(1,128)} %bitcast.8, f32[2,128,128]{2,1,0:T(8,128)} %constant.16.clone.fourier_ref, f32[2,128,128]{2,1,0:T(8,128)} %constant.17.clone.dither_ref, f32[1,128,256]{2,1,0:T(8,128)} %real_ref.1, f32[1,128,256]{2,1,0:T(8,128)} %imag_ref.1), custom_call_target="tpu_custom_call" | custom-call | tf_op jit(solution)/shard_map/prepare/pallas_call | solution.py:57
  20.7 0.0 copy-done
  20.8 0.0 collective-permute-done.real_below
  20.8 0.0 collective-permute-done.1.imag_below
  20.8 0.0 copy-start.2
  20.8 0.9 copy-done.2
  21.7 1.8 %cut.1 = f32[16,256,128]{2,1,0:T(8,128)S(1)} custom-call(s32[16,2]{1,0:T(8,128)S(1)} %copy.16.offset_ref, f32[2,2,128,128]{3,2,1,0:T(8,128)S(1)} %copy-done.2, f32[1,128,256]{2,1,0:T(8,128)S(1)} %collective-permute-done.real_below, f32[1,128,256]{2,1,0:T(8,128)S(1)} %collective-permute-done.1.imag_below), custom_call_target="tpu_custom_call" | custom-call | tf_op jit(solution)/shard_map/cut/pallas_call | solution.py:199
  23.5 0.0 copy-start.1
  23.5 0.0 copy-start.3
  23.5 0.0 copy-start.4
  23.6 59.8 %all_to_all.15.refs_2_ = f32[16,256,128]{2,1,0:T(8,128)S(1)} all-to-all(f32[16,256,128]{2,1,0:T(8,128)S(1)} %cut.1), channel_id=1, replica_groups=mesh['cuts'=16,'tile'=32] {'cuts'}, dimensions={0} | all-to-all | bytes 4194304 | tf_op jit(solution)/shard_map/all_to_all | solution.py:269
  83.4 0.0 copy-done.1
  83.4 0.0 copy-done.3
  83.4 0.0 copy-done.4
  83.4 13.8 %chain.1 = f32[16,272,128]{2,1,0:T(8,128)S(1)} custom-call(s32[1]{0:T(128)S(6)} %convert_element_type.3.live_ref, f32[128,128]{1,0:T(8,128)S(1)} %copy-done.3, f32[128,128]{1,0:T(8,128)S(1)} %copy-done.4, bf16[12,128,128]{2,1,0:T(8,128)(2,1)S(1)} %copy-done.1, f32[1,128,128]{2,1,0:T(8,128)S(1)} %constant_dynamic-slice_fusion.refs_1_, ...), custom_call_target="tpu_custom_call" | custom-call | tf_op jit(solution)/shard_map/chain/pallas_call | solution.py:155
  97.1 55.5 %all_to_all.16.terms_ref = f32[16,272,128]{2,1,0:T(8,128)S(1)} all-to-all(f32[16,272,128]{2,1,0:T(8,128)S(1)} %chain.1), channel_id=1, replica_groups=mesh['cuts'=16,'tile'=32] {'cuts'}, dimensions={0} | all-to-all | bytes 4456448 | tf_op jit(solution)/shard_map/all_to_all | solution.py:271
  152.7 0.7 broadcast_in_dim.14
  153.4 5.9 %all-to-all-start.2 = ((f32[32,16,128]{2,1,0:T(8,128)}), f32[32,16,128]{2,1,0:T(8,128)S(1)}, u32[]{:S(2)}, u32[]{:S(2)}) async-start(f32[32,16,128]{2,1,0:T(8,128)} %broadcast_in_dim.14), calls=%async_computation.2 | async-start | bytes 524288 | tf_op jit(solution)/shard_map/all_to_all | solution.py:275
  159.3 1.9 %gather.1 = (f32[2,128,256]{2,1,0:T(8,128)S(1)}, f32[2,128,256]{2,1,0:T(8,128)S(1)}) custom-call(s32[16,2]{1,0:T(8,128)S(1)} %copy.16.offset_ref, f32[16,272,128]{2,1,0:T(8,128)S(1)} %all_to_all.16.terms_ref), custom_call_target="tpu_custom_call" | custom-call | tf_op jit(solution)/shard_map/gather/pallas_call | solution.py:237
  161.2 3.1 %collective-permute-start.2 = (f32[2,128,256]{2,1,0:T(8,128)S(1)}, f32[2,128,256]{2,1,0:T(8,128)S(1)}, u32[]{:S(2)}, u32[]{:S(2)}) collective-permute-start(f32[2,128,256]{2,1,0:T(8,128)S(1)} %get-tuple-element.21), channel_id=1, source_target_pairs={{31,0},{0,1},{1,2},{2,3},{3,4},{4,5},{5,6},{6,7},{7,8},{8,9},{9,10... | collective-permute-start | bytes 786440 | tf_op jit(solution)/shard_map/ppermute | solution.py:253
  164.4 12.0 %collective-permute-done.2 = f32[2,128,256]{2,1,0:T(8,128)S(1)} collective-permute-done((f32[2,128,256]{2,1,0:T(8,128)S(1)}, f32[2,128,256]{2,1,0:T(8,128)S(1)}, u32[]{:S(2)}, u32[]{:S(2)}) %collective-permute-start.2) | collective-permute-done | bytes 262176 | tf_op jit(solution)/shard_map/ppermute | solution.py:253
  176.3 0.7 add_bitcast_fusion
  177.1 0.0 all-to-all-done.2
  177.1 0.6 reduce_sum.19
  (2 shorter events, 0.0 us)
Async XLA Ops:
  0.6 20.1 %copy-start = (f32[16,128,128]{2,1,0:T(8,128)S(1)}, f32[16,128,128]{2,1,0:T(8,128)}, u32[]{:S(2)}) copy-start(f32[16,128,128]{2,1,0:T(8,128)} %param.15) | copy-start | bytes 3145732
  0.6 20.1 %collective-permute-start = (f32[1,128,256]{2,1,0:T(8,128)}, f32[1,128,256]{2,1,0:T(8,128)S(1)}, u32[]{:S(2)}, u32[]{:S(2)}) collective-permute-start(f32[1,128,256]{2,1,0:T(8,128)} %real_ref.1), channel_id=1, source_target_pairs={{1,0},{2,1},{3,2},{4,3},{5,4},{6,5},{7,6},{8,7},{9,8},{10,9},{11,1... | collective-permute-start | bytes 393224 | tf_op jit(solution)/shard_map/ppermute | solution.py:253
  14.5 6.3 %collective-permute-start.1 = (f32[1,128,256]{2,1,0:T(8,128)}, f32[1,128,256]{2,1,0:T(8,128)S(1)}, u32[]{:S(2)}, u32[]{:S(2)}) collective-permute-start(f32[1,128,256]{2,1,0:T(8,128)} %imag_ref.1), channel_id=1, source_target_pairs={{1,0},{2,1},{3,2},{4,3},{5,4},{6,5},{7,6},{8,7},{9,8},{10,9},{11,1... | collective-permute-start | bytes 393224 | tf_op jit(solution)/shard_map/ppermute | solution.py:253
  20.8 1.0 copy-start.2
  23.5 59.8 %copy-start.1 = (bf16[12,128,128]{2,1,0:T(8,128)(2,1)S(1)}, bf16[12,128,128]{2,1,0:T(8,128)(2,1)}, u32[]{:S(2)}) copy-start(bf16[12,128,128]{2,1,0:T(8,128)(2,1)} %get-tuple-element.15.refs_0_) | copy-start | bytes 1179652
  23.5 59.8 %copy-start.3 = (f32[128,128]{1,0:T(8,128)S(1)}, f32[128,128]{1,0:T(8,128)}, u32[]{:S(2)}) copy-start(f32[128,128]{1,0:T(8,128)} %probe_real.1) | copy-start | bytes 196612
  23.5 59.8 %copy-start.4 = (f32[128,128]{1,0:T(8,128)S(1)}, f32[128,128]{1,0:T(8,128)}, u32[]{:S(2)}) copy-start(f32[128,128]{1,0:T(8,128)} %probe_imag.1) | copy-start | bytes 196612
  153.4 23.7 %all-to-all-start.2 = ((f32[32,16,128]{2,1,0:T(8,128)}), f32[32,16,128]{2,1,0:T(8,128)S(1)}, u32[]{:S(2)}, u32[]{:S(2)}) async-start(f32[32,16,128]{2,1,0:T(8,128)} %broadcast_in_dim.14), calls=%async_computation.2 | async-start | bytes 524288 | tf_op jit(solution)/shard_map/all_to_all | solution.py:275
  161.2 15.1 %collective-permute-start.2 = (f32[2,128,256]{2,1,0:T(8,128)S(1)}, f32[2,128,256]{2,1,0:T(8,128)S(1)}, u32[]{:S(2)}, u32[]{:S(2)}) collective-permute-start(f32[2,128,256]{2,1,0:T(8,128)S(1)} %get-tuple-element.21), channel_id=1, source_target_pairs={{31,0},{0,1},{1,2},{2,3},{3,4},{4,5},{5,6},{6,7},{7,8},{8,9},{9,10... | collective-permute-start | bytes 786440 | tf_op jit(solution)/shard_map/ppermute | solution.py:253

commit v5 on v4

--- a/solution.py
+++ b/solution.py
@@ -94,7 +94,10 @@
         )
         for half in split_bf16(middle)
     )
-    out = dot(left_high, high) + dot(left_low, high) + dot(left_high, low)
+    out = dot(
+        jnp.concatenate([left_high, left_low, left_high], axis=1),
+        jnp.concatenate([high, high, low], axis=0),
+    )
     return out[:, :size], out[:, size:]
 
 
@@ -248,6 +251,26 @@
     )(offsets, terms)
 
 
+def finish_kernel(own_ref, band_ref, parts_ref, object_ref, probe_ref):
+    object_ref[...] = own_ref[...] + band_ref[...]
+    probe_ref[...] = jnp.sum(parts_ref[...], axis=0)
+
+
+def finish(own, band, parts):
+    vmem = pl.BlockSpec(memory_space=VMEM)
+    return pl.pallas_call(
+        finish_kernel,
+        out_shape=[
+            jax.ShapeDtypeStruct(own.shape, jnp.float32),
+            jax.ShapeDtypeStruct(parts.shape[1:], jnp.float32),
+        ],
+        in_specs=[vmem] * 3,
+        out_specs=[vmem] * 2,
+        compiler_params=pltpu.CompilerParams(vmem_limit_bytes=12 * 2**20),
+        name="finish",
+    )(own, band, parts)
+
+
 def passed_along(block, axis, distance):
     count = lax.axis_size(axis)
     return lax.ppermute(block, axis, [((i - distance) % count, i) for i in range(count)])
@@ -275,9 +298,8 @@
     probe_parts = lax.all_to_all(spread, "tile", 0, 0, tiled=True)
     own, band = add_windows(offsets, terms, rows, width)
     band = passed_along(band, "tile", 1)
-    probe_grad = jnp.sum(probe_parts, axis=0).reshape(2, -1, size)
-    object_grad = (own + band)[:, None]
-    return object_grad, probe_grad
+    object_grad, probe_grad = finish(own, band, probe_parts)
+    return object_grad[:, None], probe_grad.reshape(2, -1, size)
 
 
 def solution(mesh):

time: 178 us -> 179 us (level)
  transfers between devices with their start and end apart: 4 -> 4, of which waited for: 1 -> 1; matrix products, arithmetic and copies ran while one was open for 1% -> 0% of each run, Pallas kernels for 2% -> 2%
where the time goes in v5:
time: 179 us; the launch traced here: 178 us
  blocking collectives  115 us (64%)
  starting transfers between devices  25.2 us (14%)
  Pallas kernels  20.5 us (11%)
  waiting for transfers between devices  11.5 us (6%)
  local copies, waits for them, and re-layouts  4.1 us (2%)
    all_to_all x1, blocking collectives, per_device(): windows = lax.all_to_all(windows, 'cuts', 0, 0, tiled=True)  59.8 us
    all_to_all x1, blocking collectives, per_device(): terms = lax.all_to_all(terms, 'cuts', 0, 0, tiled=True)  55.6 us
    ppermute x3, starting transfers between devices, passed_along(): lax.ppermute(block, axis, [((i - distance) % count, i) for i in range(cou...  19.4 us
    pallas_call x1, Pallas kernels, run_chain(): pl.pallas_call(chain_kernel, out_shape=jax.ShapeDtypeStruct((slices, rows...  13.8 us
    ppermute x3, waiting for transfers between devices, passed_along(): lax.ppermute(block, axis, [((i - distance) % count, i) for i in range(cou...  11.5 us
    all_to_all x1, starting transfers between devices, per_device(): probe_parts = lax.all_to_all(spread, 'tile', 0, 0, tiled=True)  5.8 us
  transfers between devices with their start and end apart: 4, of which 1 were waited for; matrix products, arithmetic and copies ran while one was open for 0% of the time, Pallas kernels for 2%

profile of v5, /device:TPU:1, one launch (start us, length us, event | category | flops | bytes accessed | tf_op | source)
XLA Modules:
  0.0 178.1 jit_solution(1994147016235771320)
XLA Ops:
  0.6 0.0 copy-start
  0.6 13.8 %collective-permute-start = (f32[1,128,256]{2,1,0:T(8,128)}, f32[1,128,256]{2,1,0:T(8,128)S(1)}, u32[]{:S(2)}, u32[]{:S(2)}) collective-permute-start(f32[1,128,256]{2,1,0:T(8,128)} %real_ref.1), channel_id=1, source_target_pairs={{1,0},{2,1},{3,2},{4,3},{5,4},{6,5},{7,6},{8,7},{9,8},{10,9},{11,1... | collective-permute-start | bytes 393224 | tf_op jit(solution)/shard_map/ppermute | solution.py:276
  14.5 2.5 %collective-permute-start.1 = (f32[1,128,256]{2,1,0:T(8,128)}, f32[1,128,256]{2,1,0:T(8,128)S(1)}, u32[]{:S(2)}, u32[]{:S(2)}) collective-permute-start(f32[1,128,256]{2,1,0:T(8,128)} %imag_ref.1), channel_id=1, source_target_pairs={{1,0},{2,1},{3,2},{4,3},{5,4},{6,5},{7,6},{8,7},{9,8},{10,9},{11,1... | collective-permute-start | bytes 393224 | tf_op jit(solution)/shard_map/ppermute | solution.py:276
  17.6 0.8 copy.13.offset_ref
  18.4 2.4 %prepare.1 = (bf16[12,128,128]{2,1,0:T(8,128)(2,1)}, f32[2,2,128,128]{3,2,1,0:T(8,128)}) custom-call(f32[1,128]{1,0:T(1,128)} %bitcast.6, f32[2,128,128]{2,1,0:T(8,128)} %constant.16.clone.fourier_ref, f32[2,128,128]{2,1,0:T(8,128)} %constant.17.clone.dither_ref, f32[1,128,256]{2,1,0:T(8,128)} %real_ref.1, f32[1,128,256]{2,1,0:T(8,128)} %imag_ref.1), custom_call_target="tpu_custom_call" | custom-call | tf_op jit(solution)/shard_map/prepare/pallas_call | solution.py:57
  20.7 0.0 copy-done
  20.7 0.0 collective-permute-done.real_below
  20.7 0.0 collective-permute-done.1.imag_below
  20.8 0.0 copy-start.4
  20.8 0.9 copy-done.4
  21.7 1.8 %cut.1 = f32[16,256,128]{2,1,0:T(8,128)S(1)} custom-call(s32[16,2]{1,0:T(8,128)S(1)} %copy.13.offset_ref, f32[2,2,128,128]{3,2,1,0:T(8,128)S(1)} %copy-done.4, f32[1,128,256]{2,1,0:T(8,128)S(1)} %collective-permute-done.real_below, f32[1,128,256]{2,1,0:T(8,128)S(1)} %collective-permute-done.1.imag_below), custom_call_target="tpu_custom_call" | custom-call | tf_op jit(solution)/shard_map/cut/pallas_call | solution.py:202
  23.5 0.0 copy-start.1
  23.5 0.0 copy-start.5
  23.5 0.0 copy-start.6
  23.5 59.8 %all_to_all.15.refs_2_ = f32[16,256,128]{2,1,0:T(8,128)S(1)} all-to-all(f32[16,256,128]{2,1,0:T(8,128)S(1)} %cut.1), channel_id=1, replica_groups=mesh['cuts'=16,'tile'=32] {'cuts'}, dimensions={0} | all-to-all | bytes 4194304 | tf_op jit(solution)/shard_map/all_to_all | solution.py:292
  83.4 0.0 copy-done.1
  83.4 0.0 copy-done.5
  83.4 0.0 copy-done.6
  83.4 13.8 %chain.1 = f32[16,272,128]{2,1,0:T(8,128)S(1)} custom-call(s32[1]{0:T(128)S(6)} %convert_element_type.3.live_ref, f32[128,128]{1,0:T(8,128)S(1)} %copy-done.5, f32[128,128]{1,0:T(8,128)S(1)} %copy-done.6, bf16[12,128,128]{2,1,0:T(8,128)(2,1)S(1)} %copy-done.1, f32[1,128,128]{2,1,0:T(8,128)S(1)} %constant_dynamic-slice_fusion.refs_1_, ...), custom_call_target="tpu_custom_call" | custom-call | tf_op jit(solution)/shard_map/chain/pallas_call | solution.py:158
  97.1 55.6 %all_to_all.16.terms_ref = f32[16,272,128]{2,1,0:T(8,128)S(1)} all-to-all(f32[16,272,128]{2,1,0:T(8,128)S(1)} %chain.1), channel_id=1, replica_groups=mesh['cuts'=16,'tile'=32] {'cuts'}, dimensions={0} | all-to-all | bytes 4456448 | tf_op jit(solution)/shard_map/all_to_all | solution.py:294
  152.7 0.7 broadcast_in_dim.13
  153.5 5.8 %all-to-all-start.2 = ((f32[32,16,128]{2,1,0:T(8,128)}), f32[32,16,128]{2,1,0:T(8,128)S(1)}, u32[]{:S(2)}, u32[]{:S(2)}) async-start(f32[32,16,128]{2,1,0:T(8,128)} %broadcast_in_dim.13), calls=%async_computation.2 | async-start | bytes 524288 | tf_op jit(solution)/shard_map/all_to_all | solution.py:298
  159.3 1.9 %gather.1 = (f32[2,128,256]{2,1,0:T(8,128)S(1)}, f32[2,128,256]{2,1,0:T(8,128)S(1)}) custom-call(s32[16,2]{1,0:T(8,128)S(1)} %copy.13.offset_ref, f32[16,272,128]{2,1,0:T(8,128)S(1)} %all_to_all.16.terms_ref), custom_call_target="tpu_custom_call" | custom-call | tf_op jit(solution)/shard_map/gather/pallas_call | solution.py:240
  161.1 0.0 copy-start.2
  161.2 0.7 copy-done.2
  161.9 3.1 %collective-permute-start.2 = (f32[2,128,256]{2,1,0:T(8,128)S(1)}, f32[2,128,256]{2,1,0:T(8,128)S(1)}, u32[]{:S(2)}, u32[]{:S(2)}) collective-permute-start(f32[2,128,256]{2,1,0:T(8,128)S(1)} %get-tuple-element.23), channel_id=1, source_target_pairs={{31,0},{0,1},{1,2},{2,3},{3,4},{4,5},{5,6},{6,7},{7,8},{8,9},{9,10... | collective-permute-start | bytes 786440 | tf_op jit(solution)/shard_map/ppermute | solution.py:276
  165.0 11.4 %collective-permute-done.2.band_ref = f32[2,128,256]{2,1,0:T(8,128)S(1)} collective-permute-done((f32[2,128,256]{2,1,0:T(8,128)S(1)}, f32[2,128,256]{2,1,0:T(8,128)S(1)}, u32[]{:S(2)}, u32[]{:S(2)}) %collective-permute-start.2) | collective-permute-done | bytes 262176 | tf_op jit(solution)/shard_map/ppermute | solution.py:276
  176.4 0.0 all-to-all-done.2.parts_ref
  176.4 0.0 copy-start.3
  176.4 0.9 copy-done.3
  177.4 0.7 finish.1
  (2 shorter events, 0.0 us)
Async XLA Ops:
  0.6 20.1 %copy-start = (f32[16,128,128]{2,1,0:T(8,128)S(1)}, f32[16,128,128]{2,1,0:T(8,128)}, u32[]{:S(2)}) copy-start(f32[16,128,128]{2,1,0:T(8,128)} %param.15) | copy-start | bytes 3145732
  0.6 20.1 %collective-permute-start = (f32[1,128,256]{2,1,0:T(8,128)}, f32[1,128,256]{2,1,0:T(8,128)S(1)}, u32[]{:S(2)}, u32[]{:S(2)}) collective-permute-start(f32[1,128,256]{2,1,0:T(8,128)} %real_ref.1), channel_id=1, source_target_pairs={{1,0},{2,1},{3,2},{4,3},{5,4},{6,5},{7,6},{8,7},{9,8},{10,9},{11,1... | collective-permute-start | bytes 393224 | tf_op jit(solution)/shard_map/ppermute | solution.py:276
  14.5 6.3 %collective-permute-start.1 = (f32[1,128,256]{2,1,0:T(8,128)}, f32[1,128,256]{2,1,0:T(8,128)S(1)}, u32[]{:S(2)}, u32[]{:S(2)}) collective-permute-start(f32[1,128,256]{2,1,0:T(8,128)} %imag_ref.1), channel_id=1, source_target_pairs={{1,0},{2,1},{3,2},{4,3},{5,4},{6,5},{7,6},{8,7},{9,8},{10,9},{11,1... | collective-permute-start | bytes 393224 | tf_op jit(solution)/shard_map/ppermute | solution.py:276
  20.8 1.0 copy-start.4
  23.5 59.9 %copy-start.1 = (bf16[12,128,128]{2,1,0:T(8,128)(2,1)S(1)}, bf16[12,128,128]{2,1,0:T(8,128)(2,1)}, u32[]{:S(2)}) copy-start(bf16[12,128,128]{2,1,0:T(8,128)(2,1)} %get-tuple-element.17.refs_0_) | copy-start | bytes 1179652
  23.5 59.8 %copy-start.5 = (f32[128,128]{1,0:T(8,128)S(1)}, f32[128,128]{1,0:T(8,128)}, u32[]{:S(2)}) copy-start(f32[128,128]{1,0:T(8,128)} %probe_real.1) | copy-start | bytes 196612
  23.5 59.8 %copy-start.6 = (f32[128,128]{1,0:T(8,128)S(1)}, f32[128,128]{1,0:T(8,128)}, u32[]{:S(2)}) copy-start(f32[128,128]{1,0:T(8,128)} %probe_imag.1) | copy-start | bytes 196612
  153.5 23.0 %all-to-all-start.2 = ((f32[32,16,128]{2,1,0:T(8,128)}), f32[32,16,128]{2,1,0:T(8,128)S(1)}, u32[]{:S(2)}, u32[]{:S(2)}) async-start(f32[32,16,128]{2,1,0:T(8,128)} %broadcast_in_dim.13), calls=%async_computation.2 | async-start | bytes 524288 | tf_op jit(solution)/shard_map/all_to_all | solution.py:298
  161.1 0.7 copy-start.2
  161.9 14.6 %collective-permute-start.2 = (f32[2,128,256]{2,1,0:T(8,128)S(1)}, f32[2,128,256]{2,1,0:T(8,128)S(1)}, u32[]{:S(2)}, u32[]{:S(2)}) collective-permute-start(f32[2,128,256]{2,1,0:T(8,128)S(1)} %get-tuple-element.23), channel_id=1, source_target_pairs={{31,0},{0,1},{1,2},{2,3},{3,4},{4,5},{5,6},{6,7},{7,8},{8,9},{9,10... | collective-permute-start | bytes 786440 | tf_op jit(solution)/shard_map/ppermute | solution.py:276
  176.4 1.0 copy-start.3
